TPU v7x, 128 devices: a whole 4x4x4 slice. The times are simulated.
128 devices in a mesh: row: 8 (over y, core), col: 16 (over x, z).
Axes of the slice: x: 4, y: 4, z: 4, core: 2. Of those that a mesh axis runs over, the one named last changes fastest.
Arguments:
- features: bfloat16 [65536, 128], P(('col', 'row')), may hold values from -6 to 6
- weight: bfloat16 [128, 128], replicated, may hold values from -0.5 to 0.5
- adjacency: bfloat16 [8, 16, 512, 128, 128], P('row', 'col'), may hold values from -0.046875 to 0.046875
- row_index: int32 [8, 16, 512], P('row', 'col'), may hold values from 0 to 63
- col_index: int32 [8, 16, 512], P('row', 'col'), may hold values from 0 to 31
- block_count: int32 [8, 16], P('row', 'col'), may hold values from 170 to 512, as said below
- grad_out: bfloat16 [65536, 128], P(('row', 'col')), may hold values from -6 to 6
Outputs:
- activated: bfloat16 [65536, 128], P(('row', 'col'))
- input_grad: bfloat16 [65536, 128], P(('col', 'row'))
- weight_grad: float32 [128, 128], replicated
Inputs may be any that keep to these rules, and one draw needn't show every extreme that they name: `block_count`: slots at or beyond a position's count hold arbitrary values and indices and are ignored; some position holds exactly 512 live slots in every draw. `row_index`: several slots may name the same block; their values add.
All inputs are finite; a program needn't handle non-finite values.
Results may differ from a plain program's by a relative error of at most 0.0075.
Values may be sent and summed in bfloat16 or wider, within the bound.
No kernel may reach another device: no remote copies, remote signals or barrier semaphores. Data moves between devices by JAX's collectives and lax.ppermute only.
A program may use at most 192 MiB of HBM per device.

v0:
```python
import functools

import jax
import jax.numpy as jnp
from jax import lax
from jax.experimental import pallas as pl
from jax.experimental.pallas import tpu as pltpu
from jax.sharding import PartitionSpec as P

BLK = 128
NX = 4
NZ = 4
NY = 4
ROW_BLOCKS = 64
COL_BLOCKS = 32
OWN = 4
F32 = jnp.float32
BF16 = jnp.bfloat16
VMEM_LIMIT = 24 * 1024 * 1024


def vmem_specs(n):
    return [pl.BlockSpec(memory_space=pltpu.VMEM)] * n


def params():
    return pltpu.CompilerParams(vmem_limit_bytes=VMEM_LIMIT)


FAR_F, TWO_F, REST_F, EARLY_B, OTHER_B, OWN_B = range(6)
LISTS = 6
FAR = (NZ - 1) * OWN
OTHER = NY * OWN


def prepare_kernel(packed_ref, adj_ref, blocks_ref, *refs):
    codes_refs, sem = refs[:-1], refs[-1]
    copy = pltpu.make_async_copy(adj_ref, blocks_ref, sem)
    copy.start()
    row, col = lax.axis_index("row"), lax.axis_index("col")
    y, core = row >> 1, row & 1
    x, z = col >> 2, col & 3
    packed = packed_ref[...]
    alive = packed >= 0
    brow, bcol = packed & (ROW_BLOCKS - 1), packed >> 6
    capacity = packed.shape[1]
    slot = lax.broadcasted_iota(jnp.int32, (1, capacity), 1)
    rx, rz, rb = (brow >> 4) & 3, (brow >> 2) & 3, brow & 3
    cy, cc, cb = (bcol >> 3) & 3, (bcol >> 2) & 1, bcol & 3
    ahead, behind, up = (rx - x) & 3, (x - rx) & 3, (cy - y) & 3
    ahead_z, behind_z = (rz - z) & 3, (z - rz) & 3
    other = cc ^ core
    odd, level = ahead & 1, ahead_z == 0
    far = (odd == 1) & (ahead_z > 0)
    rest = (ahead == 0) | ((odd == 1) & level)
    near_row = jnp.where(odd == 1, NZ * OWN + (ahead >> 1) * OWN + rb, ahead_z * OWN + rb)
    to_row = jnp.where(far, (ahead >> 1) * FAR + (ahead_z - 1) * OWN + rb, near_row)
    near_row = jnp.where(odd == 1, NZ * OWN + (behind >> 1) * OWN + rb, behind_z * OWN + rb)
    near_row = jnp.where((ahead == 2) & level, (NZ + 2) * OWN + rb, near_row)
    near_row = jnp.where((ahead == 2) & (ahead_z > 0), near_row - OWN, near_row)
    from_row = jnp.where(far, FAR + (behind >> 1) * FAR + (behind_z - 1) * OWN + rb, near_row)
    to_col = jnp.where((rest | ((ahead == 2) & level)) & (other == 0), OTHER, 0) + up * OWN + cb
    from_col = other * 16 + ((y - cy) & 3) * OWN + cb
    forward_kind = jnp.where(rest, 2, jnp.where(far, 0, 1))
    forward_kind = jnp.where(alive, forward_kind, 3)
    early = rest | ((ahead == 2) & level)
    backward_kind = jnp.where(early, 2, 1 - other)
    backward_kind = jnp.where(alive, backward_kind, 3)
    row_codes = [
        (slot + 512 * to_row + 65536 * from_col).astype(F32),
        (slot + 512 * to_col + 65536 * from_row).astype(F32),
        forward_kind.astype(F32),
        backward_kind.astype(F32),
    ]
    member = [(forward_kind == k).astype(F32) for k in range(3)] + [(backward_kind == k).astype(F32) for k in range(3)]
    counts = [jnp.sum(m, axis=1, keepdims=True) for m in member]
    lists = [jnp.zeros((1, capacity), F32) for _ in range(LISTS)]
    step = 64
    lane = lax.broadcasted_iota(jnp.int32, (step, capacity), 1)
    place = lane.astype(F32)
    for c in range(0, capacity, step):
        sub = lax.broadcasted_iota(jnp.int32, (step, capacity), 0) + c
        fcode, bcode, fkind, bkind = (
            jnp.sum(jnp.where(lane == sub, v, 0.0), axis=1, keepdims=True) for v in row_codes
        )
        ranks = [
            jnp.sum(jnp.where(lane <= sub, m, 0.0), axis=1, keepdims=True) - 1.0 for m in member
        ]
        kinds = [(fkind, 0.0), (fkind, 1.0), (fkind, 2.0), (bkind, 0.0), (bkind, 1.0), (bkind, 2.0)]
        ranks = [jnp.where(kind == k, r, -1.0) for (kind, k), r in zip(kinds, ranks)]
        for q, rank, code in (
            (FAR_F, ranks[0], fcode),
            (TWO_F, ranks[1], fcode),
            (REST_F, ranks[2], fcode),
            (EARLY_B, ranks[5], bcode),
            (OTHER_B, ranks[3], bcode),
            (OWN_B, ranks[4], bcode),
        ):
            lists[q] += jnp.sum(jnp.where(place == rank, code, 0.0), axis=0, keepdims=True)
    where = slot.astype(F32)
    for q, count, idle in (
        (FAR_F, counts[0], 2 * FAR),
        (TWO_F, counts[1], NZ * OWN),
        (REST_F, counts[2], (NZ + 2) * OWN),
        (EARLY_B, counts[5], COL_BLOCKS),
        (OTHER_B, counts[3], OTHER),
        (OWN_B, counts[4], OTHER),
    ):
        codes_refs[q][:, 0:capacity] = jnp.where(where < count, lists[q], 512.0 * idle).astype(jnp.int32)
        codes_refs[q][:, capacity : capacity + BLK] = jnp.broadcast_to(count, (1, BLK)).astype(jnp.int32)
    copy.wait()


def prepare(adjacency, packed):
    capacity = adjacency.shape[0]
    return pl.pallas_call(
        prepare_kernel,
        out_shape=[
            jax.ShapeDtypeStruct(adjacency.shape, adjacency.dtype),
        ]
        + [jax.ShapeDtypeStruct((1, capacity + BLK), jnp.int32)] * LISTS,
        in_specs=vmem_specs(1) + [pl.BlockSpec(memory_space=pl.ANY)],
        out_specs=vmem_specs(1 + LISTS),
        scratch_shapes=[pltpu.SemaphoreType.DMA],
        compiler_params=params(),
        cost_estimate=pl.CostEstimate(flops=0, bytes_accessed=2 * adjacency.size * 2, transcendentals=0),
        name="prepare",
    )(packed, adjacency)


def accumulate(unroll, codes_ref, acc, product):
    @pl.loop(0, pl.cdiv(codes_ref[0, codes_ref.shape[1] - BLK], unroll))
    def _(g):
        codes = [codes_ref[0, g * unroll + j] for j in range(unroll)]
        prods = [product(c & 511, c >> 16) for c in codes]
        for j in range(unroll):
            acc[(codes[j] >> 9) & 127] += prods[j]


def sparse_cost(share):
    return pl.CostEstimate(
        flops=int(512 * BLK**3 * 8 * share), bytes_accessed=int(20 * 2**20 * share), transcendentals=0
    )


def sparse_call(kernel, codes, adjacency, operands, outs, scratch, share, name):
    return pl.pallas_call(
        kernel,
        out_shape=[jax.ShapeDtypeStruct(shape, dtype) for shape, dtype in outs],
        in_specs=[pl.BlockSpec(memory_space=pltpu.SMEM)] + vmem_specs(1 + len(operands)),
        out_specs=vmem_specs(len(outs)),
        scratch_shapes=[pltpu.VMEM((blocks, BLK, BLK), dtype) for blocks, dtype in scratch],
        compiler_params=params(),
        cost_estimate=sparse_cost(share),
        name=name,
    )(codes, adjacency, *operands)


def write_rows(acc, outs):
    at = 0
    for out in outs:
        blocks = out.shape[0] // BLK
        out[...] = acc[pl.ds(at, blocks)].reshape(out.shape).astype(out.dtype)
        at += blocks


def forward_far_kernel(nin, codes_ref, adj_ref, *refs):
    ins, (feats, *outs), acc = refs[:nin], refs[nin:-1], refs[-1]
    per = feats.shape[0] // nin
    for i in range(nin):
        feats[pl.ds(i * per, per)] = ins[i][...].reshape(per, BLK, BLK)
    acc[...] = jnp.zeros_like(acc)

    def product(slot, source):
        return jnp.dot(adj_ref[slot], feats[source], preferred_element_type=F32)

    accumulate(64, codes_ref, acc, product)
    write_rows(acc, outs)


def forward_near_kernel(unroll, codes_ref, adj_ref, feats, *refs):
    outs, acc = refs[:-1], refs[-1]
    acc[...] = jnp.zeros_like(acc)

    def product(slot, source):
        return jnp.dot(adj_ref[slot], feats[source], preferred_element_type=F32)

    accumulate(unroll, codes_ref, acc, product)
    write_rows(acc, outs)


def gather_slopes(slopes, ins):
    at = 0
    for part in ins:
        blocks = part.shape[0] // BLK - 1
        slopes[pl.ds(at, blocks)] = part[pl.ds(0, blocks * BLK)].reshape(blocks, BLK, BLK)
        at += blocks


def last_block(part):
    return part[pl.ds(part.shape[0] - BLK, BLK)].astype(F32)


def backward_early_kernel(nin, codes_ref, adj_ref, *refs):
    ins, acc, slopes = refs[:nin], refs[nin], refs[nin + 1]
    gather_slopes(slopes, ins)
    acc[...] = jnp.zeros_like(acc)

    def product(slot, source):
        return jnp.dot(slopes[source], adj_ref[slot], preferred_element_type=F32)

    accumulate(64, codes_ref, acc, product)


def backward_other_kernel(nin, codes_ref, adj_ref, before, rest, level, *refs):
    ins, (send, wsum, slopes), acc = refs[:nin], refs[nin : nin + 3], refs[-1]
    gather_slopes(slopes, ins)
    acc[...] = before[pl.ds(0, OTHER + 1)]

    def product(slot, source):
        return jnp.dot(slopes[source], adj_ref[slot], preferred_element_type=F32)

    accumulate(64, codes_ref, acc, product)
    send[pl.ds(0, OTHER * BLK)] = acc[pl.ds(0, OTHER)].reshape(OTHER * BLK, BLK)
    total = last_block(rest) + last_block(level) + sum(last_block(part) for part in ins)
    wsum[...] = total
    send[pl.ds(OTHER * BLK, BLK)] = total


def backward_own_kernel(codes_ref, adj_ref, before, slopes, keep, acc):
    acc[...] = before[pl.ds(OTHER, OTHER + 1)]

    def product(slot, source):
        return jnp.dot(slopes[source], adj_ref[slot], preferred_element_type=F32)

    accumulate(64, codes_ref, acc, product)
    keep[...] = acc[pl.ds(0, OTHER)].reshape(keep.shape)


def add_split_kernel(nin, *refs):
    ins, outs = refs[:nin], refs[nin:]
    at = 0
    for out in outs:
        rows = out.shape[0]
        total = ins[0][pl.ds(at, rows)].astype(F32)
        for part in ins[1:]:
            total += part[pl.ds(at, rows)].astype(F32)
        out[...] = total.astype(out.dtype)
        at += rows


def add_split(parts, dtypes, name):
    rows = parts[0].shape[0] // len(dtypes)
    return pl.pallas_call(
        functools.partial(add_split_kernel, len(parts)),
        out_shape=[jax.ShapeDtypeStruct((rows, BLK), dtype) for dtype in dtypes],
        in_specs=vmem_specs(len(parts)),
        out_specs=vmem_specs(len(dtypes)),
        compiler_params=params(),
        name=name,
    )(*parts)


def activate_kernel(weight_ref, grad_ref, *refs):
    parts, (act_ref, pay_ref) = refs[:-2], refs[-2:]
    rows = act_ref.shape[0]
    total = parts[0][...]
    for part in parts[1:]:
        total += part[...].astype(F32)
    high = total.astype(BF16)
    rest = total - high.astype(F32)
    low = rest.astype(BF16)
    lowest = (rest - low.astype(F32)).astype(BF16)
    weight = weight_ref[...]
    pre = jnp.dot(lowest, weight, preferred_element_type=F32)
    pre += jnp.dot(low, weight, preferred_element_type=F32)
    pre += jnp.dot(high, weight, preferred_element_type=F32)
    squash = jnp.tanh(pre)
    act_ref[...] = squash.astype(BF16)
    slope = (grad_ref[...].astype(F32) * (1.0 - squash * squash)).astype(BF16)
    wterm = jnp.zeros((BLK, BLK), F32)
    for b in range(0, rows, BLK):
        turned = slope[b : b + BLK].T
        pay_ref[pl.ds(b, BLK)] = turned
        wterm += jnp.dot(turned, high[b : b + BLK], preferred_element_type=F32)
        wterm += jnp.dot(turned, low[b : b + BLK], preferred_element_type=F32)
    pay_ref[pl.ds(rows, BLK)] = wterm.astype(BF16)


def activate(weight, grad_out, parts):
    rows = grad_out.shape[0]
    return pl.pallas_call(
        activate_kernel,
        out_shape=[
            jax.ShapeDtypeStruct((rows, BLK), BF16),
            jax.ShapeDtypeStruct((rows + BLK, BLK), BF16),
        ],
        in_specs=vmem_specs(2 + len(parts)),
        out_specs=vmem_specs(2),
        compiler_params=params(),
        name="activate",
    )(weight, grad_out, *parts)


def merge_kernel(own, *refs):
    parts, out = refs[:-1], refs[-1]
    rows = own.shape[0] - BLK
    total = last_block(own)
    for i, part in enumerate(parts):
        out[pl.ds(i * rows, rows)] = part[pl.ds(0, rows)]
        total += last_block(part)
    out[pl.ds(len(parts) * rows, BLK)] = total.astype(BF16)


def merge(own, parts):
    rows = len(parts) * (own.shape[0] - BLK) + BLK
    return pl.pallas_call(
        merge_kernel,
        out_shape=jax.ShapeDtypeStruct((rows, BLK), BF16),
        in_specs=vmem_specs(1 + len(parts)),
        out_specs=pl.BlockSpec(memory_space=pltpu.VMEM),
        compiler_params=params(),
        name="merge_z",
    )(own, *parts)


def add_core_kernel(keep, wkeep, got, *outs):
    parts, own, wown = outs[:-2], outs[-2], outs[-1]
    rows = own.shape[0]
    wsum = wkeep[...] + last_block(got)
    wown[...] = wsum
    own[...] = keep[pl.ds(0, rows)] + got[pl.ds(0, rows)]
    for i, part in enumerate(parts, 1):
        part[pl.ds(0, rows)] = (keep[pl.ds(i * rows, rows)] + got[pl.ds(i * rows, rows)]).astype(BF16)
        part[pl.ds(rows, BLK)] = wsum.astype(BF16)


def add_core(keep, wkeep, got):
    rows = keep.shape[0] // NY
    return pl.pallas_call(
        add_core_kernel,
        out_shape=[jax.ShapeDtypeStruct((rows + BLK, BLK), BF16)] * (NY - 1)
        + [jax.ShapeDtypeStruct((rows, BLK), F32), jax.ShapeDtypeStruct((BLK, BLK), F32)],
        in_specs=vmem_specs(3),
        out_specs=vmem_specs(NY + 1),
        compiler_params=params(),
        name="add_core",
    )(keep, wkeep, got)


def finish_kernel(scale, weight_ref, own, wown, *refs):
    parts, (out_ref, wout_ref) = refs[:-2], refs[-2:]
    rows = own.shape[0]
    total, wsum = own[...], wown[...]
    for part in parts:
        total += part[pl.ds(0, rows)].astype(F32)
        wsum += part[pl.ds(rows, BLK)].astype(F32)
    turned = total.astype(BF16)
    for b in range(0, rows, BLK):
        block = jnp.dot(weight_ref[...], turned[b : b + BLK], preferred_element_type=F32)
        out_ref[pl.ds(b, BLK)] = block.T.astype(BF16)
    wout_ref[...] = wsum.T * scale


def finish(scale, weight, own, wown, parts):
    return pl.pallas_call(
        functools.partial(finish_kernel, scale),
        out_shape=[
            jax.ShapeDtypeStruct(own.shape, BF16),
            jax.ShapeDtypeStruct((BLK, BLK), F32),
        ],
        in_specs=vmem_specs(3 + len(parts)),
        out_specs=vmem_specs(2),
        compiler_params=params(),
        name="finish",
    )(weight, own, wown, *parts)


def shift_x(a, d):
    return lax.ppermute(a, "col", [(i, (i // NZ + d) % NX * NZ + i % NZ) for i in range(NX * NZ)])


def shift_z(a, d):
    return lax.ppermute(a, "col", [(i, i // NZ * NZ + (i % NZ + d) % NZ) for i in range(NX * NZ)])


def shift_y(a, d):
    return lax.ppermute(a, "row", [(i, (i // 2 + d) % NY * 2 + i % 2) for i in range(NY * 2)])


def swap_core(a):
    return lax.ppermute(a, "row", [(i, i ^ 1) for i in range(NY * 2)])


def local(features, weight, adjacency, row_index, col_index, block_count, grad_out):
    own_rows = features.shape[0]

    beside = [shift_y(features, d) for d in range(1, NY)]
    alive = jnp.arange(adjacency.shape[2], dtype=jnp.int32)[None] < block_count
    packed = jnp.where(alive, row_index[0] + ROW_BLOCKS * col_index[0], -1)
    blocks, *codes = prepare(adjacency[0, 0], packed)
    beside, blocks, codes = lax.optimization_barrier((beside, blocks, codes))
    mine = [features] + beside
    theirs = [swap_core(a) for a in mine]

    feats, x1, x3 = sparse_call(
        functools.partial(forward_far_kernel, 2 * NY),
        codes[FAR_F],
        blocks,
        mine + theirs,
        [((COL_BLOCKS, BLK, BLK), BF16)] + [((FAR * BLK, BLK), BF16)] * 2,
        [(2 * FAR + 1, F32)],
        0.375,
        "forward_far",
    )
    x1, x3 = shift_x(x1, 1), shift_x(x3, 3)
    across, z1, z2, z3 = sparse_call(
        functools.partial(forward_near_kernel, 32),
        codes[TWO_F],
        blocks,
        [feats],
        [((own_rows, BLK), F32)] + [((own_rows, BLK), BF16)] * 3,
        [(NZ * OWN + 1, F32)],
        0.25,
        "forward_two",
    )
    z1, z2, z3 = shift_z(z1, 1), shift_z(z2, 2), shift_z(z3, 3)
    own, column, n1, n3 = sparse_call(
        functools.partial(forward_near_kernel, 64),
        codes[REST_F],
        blocks,
        [feats],
        [((own_rows, BLK), F32), ((FAR * BLK, BLK), F32)] + [((own_rows, BLK), BF16)] * 2,
        [((NZ + 2) * OWN + 1, F32)],
        0.375,
        "forward_rest",
    )
    from_z = [z1, z2, z3]
    z1, z2, z3 = add_split([column, x1, x3], [BF16] * 3, "add_x")
    across, z1, n1, n3 = lax.optimization_barrier((across, z1, n1, n3))
    z1, z2, z3 = shift_z(z1, 1), shift_z(z2, 2), shift_z(z3, 3)
    across = add_split([across] + from_z, [BF16], "add_z")[0]
    parts = [own, z1, z2, z3, shift_x(n1, 1), shift_x(n3, 3), shift_x(across, 2)]
    activated, pay = activate(weight, grad_out, parts)

    beside = [shift_z(pay, d) for d in range(1, NZ)]
    across = shift_x(pay, 2)
    n1, n3 = shift_x(pay, 1), shift_x(pay, 3)
    rest = merge(pay, beside)
    first, second = shift_x(rest, 1), shift_x(rest, 3)
    across = [across] + [shift_z(across, d) for d in range(1, NZ)]

    part = sparse_call(
        functools.partial(backward_early_kernel, 5),
        codes[EARLY_B],
        blocks,
        [pay, rest, n1, n3, across[0]],
        [((COL_BLOCKS + 1, BLK, BLK), F32)],
        [((NZ + 3) * OWN, BF16)],
        0.375,
        "backward_early",
    )[0]
    late = 3 * FAR
    send, wkeep, slopes = sparse_call(
        functools.partial(backward_other_kernel, NZ + 1),
        codes[OTHER_B],
        blocks,
        [part, rest, across[0]] + across[1:] + [first, second],
        [(((OTHER + 1) * BLK, BLK), F32), ((BLK, BLK), F32), ((late, BLK, BLK), BF16)],
        [(OTHER + 1, F32)],
        0.3,
        "backward_other",
    )
    got = swap_core(send)
    keep = sparse_call(
        backward_own_kernel,
        codes[OWN_B],
        blocks,
        [part, slopes],
        [((OTHER * BLK, BLK), F32)],
        [(OTHER + 1, F32)],
        0.3,
        "backward_own",
    )[0]
    *parts, own, wown = add_core(keep, wkeep, got)
    parts = [shift_y(part, d) for d, part in enumerate(parts, 1)]
    nodes_all = own_rows * lax.axis_size("row") * lax.axis_size("col")
    input_grad, weight_grad = finish(nodes_all ** (-0.5), weight, own, wown, parts)
    return (activated, input_grad, weight_grad)


def solution(mesh):
    placed = (
        P(("col", "row"), None),
        P(),
        P("row", "col", None, None, None),
        P("row", "col", None),
        P("row", "col", None),
        P("row", "col"),
        P(("row", "col"), None),
    )
    return jax.shard_map(
        local,
        mesh=mesh,
        in_specs=placed,
        out_specs=(P(("row", "col"), None), P(("col", "row"), None), P()),
        check_vma=False,
    )
```

profile of v0, /device:TPU:1, one launch (start us, length us, event | category | flops | bytes accessed | tf_op | source)
XLA Modules:
  0.0 92.6 jit_solution(3272335957611805451)
XLA Ops:
  0.6 3.6 %collective-permute-start.2 = (bf16[512,128]{1,0:T(8,128)(2,1)}, bf16[512,128]{1,0:T(8,128)(2,1)S(1)}, u32[]{:S(2)}, u32[]{:S(2)}) collective-permute-start(bf16[512,128]{1,0:T(8,128)(2,1)} %refs_0_.1), channel_id=1, source_target_pairs={{0,96},{16,112},{32,0},{48,16},{64,32},{80,48},{96,64},{112,80},{1... | collective-permute-start | bytes 393224 | tf_op jit(solution)/shard_map/ppermute | solution.py:388
  4.3 0.3 collective-permute-start.1
  4.6 0.7 collective-permute-start
  5.3 1.5 %collective-permute-start.3 = (bf16[512,128]{1,0:T(8,128)(2,1)}, bf16[512,128]{1,0:T(8,128)(2,1)S(1)}, u32[]{:S(2)}, u32[]{:S(2)}) collective-permute-start(bf16[512,128]{1,0:T(8,128)(2,1)} %refs_0_.1), channel_id=1, source_target_pairs={{0,16},{16,0},{32,48},{48,32},{64,80},{80,64},{96,112},{112,96},{1... | collective-permute-start | bytes 393224 | tf_op jit(solution)/shard_map/ppermute | solution.py:392
  7.5 0.7 compare_select_fusion.packed_ref
  8.2 5.8 %prepare.1 = (bf16[512,128,128]{2,1,0:T(8,128)(2,1)S(1)}, s32[1,640]{1,0:T(1,128)S(1)}, s32[1,640]{1,0:T(1,128)S(1)}, s32[1,640]{1,0:T(1,128)S(1)}, s32[1,640]{1...) custom-call(s32[1,512]{1,0:T(1,128)S(1)} %compare_select_fusion.packed_ref, bf16[512,128,128]{2,1,0:T(8,128)(2,1)} %bitcast.5), custom_call_target="tpu_custom_call" | custom-call | bytes 33554432 | tf_op jit(solution)/shard_map/prepare/pallas_call | solution.py:116
  14.0 0.0 collective-permute-done.2.refs_3_
  14.0 0.0 collective-permute-done.1.refs_2_
  14.0 0.1 collective-permute-done.refs_1_
  14.1 0.6 collective-permute-start.4
  14.7 0.0 collective-permute-start.5
  14.7 0.5 collective-permute-start.6
  15.2 0.0 collective-permute-done.3.refs_4_
  15.2 0.5 collective-permute-done.4.refs_5_
  15.7 0.4 collective-permute-done.5.refs_6_
  16.0 0.2 collective-permute-done.6.refs_7_
  16.2 3.5 %forward_far.1 = (bf16[32,128,128]{2,1,0:T(8,128)(2,1)S(1)}, bf16[1536,128]{1,0:T(8,128)(2,1)S(1)}, bf16[1536,128]{1,0:T(8,128)(2,1)S(1)}) custom-call(s32[1,640]{1,0:T(1,128)S(1)} %get-tuple-element.59.codes_ref, bf16[512,128,128]{2,1,0:T(8,128)(2,1)S(1)} %get-tuple-element.58.adj_ref, bf16[512,128]{1,0:T(8,128)(2,1)S(1)} %copy-done, ...), custom_call_target="tpu_custom_call" | custom-call | flops 3221225472 | bytes 7864320 | tf_op jit(solution)/shard_map/forward_far/pallas_call | solution.py:147
  19.7 0.4 collective-permute-start.7
  20.1 2.4 %collective-permute-start.8 = (bf16[1536,128]{1,0:T(8,128)(2,1)S(1)}, bf16[1536,128]{1,0:T(8,128)(2,1)S(1)}, u32[]{:S(2)}, u32[]{:S(2)}) collective-permute-start(bf16[1536,128]{1,0:T(8,128)(2,1)S(1)} %get-tuple-element.69), channel_id=1, source_target_pairs={{0,12},{1,13},{2,14},{3,15},{4,0},{5,1},{6,2},{7,3},{8,4},{9,5},{1... | collective-permute-start | bytes 1179656 | tf_op jit(solution)/shard_map/ppermute | solution.py:380
  22.5 2.6 %forward_two.1 = (f32[512,128]{1,0:T(8,128)S(1)}, bf16[512,128]{1,0:T(8,128)(2,1)S(1)}, bf16[512,128]{1,0:T(8,128)(2,1)S(1)}, bf16[512,128]{1,0:T(8,128)(2,1)S(1)}) custom-call(s32[1,640]{1,0:T(1,128)S(1)} %get-tuple-element.65.codes_ref, bf16[512,128,128]{2,1,0:T(8,128)(2,1)S(1)} %get-tuple-element.58.adj_ref, bf16[32,128,128]{2,1,0:T(8,128)(2,1)S(1)} %get-tuple-element.63.feats), custom_call_target="tpu_custom_call" | custom-call | flops 2147483648 | bytes 5242880 | tf_op jit(solution)/shard_map/forward_two/pallas_call | solution.py:147
  25.1 1.7 %collective-permute-start.14 = (bf16[512,128]{1,0:T(8,128)(2,1)S(1)}, bf16[512,128]{1,0:T(8,128)(2,1)S(1)}, u32[]{:S(2)}, u32[]{:S(2)}) collective-permute-start(bf16[512,128]{1,0:T(8,128)(2,1)S(1)} %get-tuple-element.79), channel_id=1, source_target_pairs={{0,1},{1,2},{2,3},{3,0},{4,5},{5,6},{6,7},{7,4},{8,9},{9,10},{10,1... | collective-permute-start | bytes 393224 | tf_op jit(solution)/shard_map/ppermute | solution.py:384
  26.8 3.3 %collective-permute-start.15 = (bf16[512,128]{1,0:T(8,128)(2,1)S(1)}, bf16[512,128]{1,0:T(8,128)(2,1)S(1)}, u32[]{:S(2)}, u32[]{:S(2)}) collective-permute-start(bf16[512,128]{1,0:T(8,128)(2,1)S(1)} %get-tuple-element.80), channel_id=1, source_target_pairs={{0,2},{1,3},{2,0},{3,1},{4,6},{5,7},{6,4},{7,5},{8,10},{9,11},{10,... | collective-permute-start | bytes 393224 | tf_op jit(solution)/shard_map/ppermute | solution.py:384
  30.1 0.1 collective-permute-start.16
  30.2 4.3 %forward_rest.1 = (f32[512,128]{1,0:T(8,128)S(1)}, f32[1536,128]{1,0:T(8,128)S(1)}, bf16[512,128]{1,0:T(8,128)(2,1)S(1)}, bf16[512,128]{1,0:T(8,128)(2,1)S(1)}) custom-call(s32[1,640]{1,0:T(1,128)S(1)} %get-tuple-element.57.codes_ref, bf16[512,128,128]{2,1,0:T(8,128)(2,1)S(1)} %get-tuple-element.58.adj_ref, bf16[32,128,128]{2,1,0:T(8,128)(2,1)S(1)} %get-tuple-element.63.feats), custom_call_target="tpu_custom_call" | custom-call | flops 3221225472 | bytes 7864320 | tf_op jit(solution)/shard_map/forward_rest/pallas_call | solution.py:147
  34.5 0.0 copy-start.1
  34.5 0.0 copy-start.2
  34.5 0.0 collective-permute-done.7.refs_1_
  34.5 0.0 collective-permute-done.8.refs_2_
  34.6 0.1 add_x.1
  34.7 0.5 collective-permute-start.9
  35.2 0.0 collective-permute-start.12
  35.2 0.0 collective-permute-done.14.refs_1_
  35.2 2.7 %collective-permute-start.13 = (bf16[512,128]{1,0:T(8,128)(2,1)S(1)}, bf16[512,128]{1,0:T(8,128)(2,1)S(1)}, u32[]{:S(2)}, u32[]{:S(2)}) collective-permute-start(bf16[512,128]{1,0:T(8,128)(2,1)S(1)} %get-tuple-element.77), channel_id=1, source_target_pairs={{0,12},{1,13},{2,14},{3,15},{4,0},{5,1},{6,2},{7,3},{8,4},{9,5},{1... | collective-permute-start | bytes 393224 | tf_op jit(solution)/shard_map/ppermute | solution.py:380
  37.9 0.1 add_z.1
  38.0 0.1 collective-permute-start.17
  38.1 3.0 %collective-permute-start.10 = (bf16[512,128]{1,0:T(8,128)(2,1)S(1)}, bf16[512,128]{1,0:T(8,128)(2,1)S(1)}, u32[]{:S(2)}, u32[]{:S(2)}) collective-permute-start(bf16[512,128]{1,0:T(8,128)(2,1)S(1)} %get-tuple-element.74), channel_id=1, source_target_pairs={{0,2},{1,3},{2,0},{3,1},{4,6},{5,7},{6,4},{7,5},{8,10},{9,11},{10,... | collective-permute-start | bytes 393224 | tf_op jit(solution)/shard_map/ppermute | solution.py:384
  41.1 0.7 collective-permute-start.11
  41.9 0.0 collective-permute-done.12.refs_4_
  41.9 1.7 %collective-permute-done.17.refs_6_ = bf16[512,128]{1,0:T(8,128)(2,1)S(1)} collective-permute-done((bf16[512,128]{1,0:T(8,128)(2,1)S(1)}, bf16[512,128]{1,0:T(8,128)(2,1)S(1)}, u32[]{:S(2)}, u32[]{:S(2)}) %collective-permute-start.17) | collective-permute-done | bytes 131104 | tf_op jit(solution)/shard_map/ppermute | solution.py:380
  43.6 1.7 %collective-permute-done.11.refs_3_ = bf16[512,128]{1,0:T(8,128)(2,1)S(1)} collective-permute-done((bf16[512,128]{1,0:T(8,128)(2,1)S(1)}, bf16[512,128]{1,0:T(8,128)(2,1)S(1)}, u32[]{:S(2)}, u32[]{:S(2)}) %collective-permute-start.11) | collective-permute-done | bytes 131104 | tf_op jit(solution)/shard_map/ppermute | solution.py:384
  45.3 1.0 %activate.1 = (bf16[512,128]{1,0:T(8,128)(2,1)}, bf16[640,128]{1,0:T(8,128)(2,1)S(1)}) custom-call(bf16[128,128]{1,0:T(8,128)(2,1)S(1)} %copy-done.2, bf16[512,128]{1,0:T(8,128)(2,1)S(1)} %copy-done.1, f32[512,128]{1,0:T(8,128)S(1)} %get-tuple-element.64.refs_0_, bf16[512,128]{1,0:T(8,128)(2,1)S(1)} %collective-permute-done.9.refs_1_, ...), custom_call_target="tpu_custom_call" | custom-call | tf_op jit(solution)/shard_map/activate/pallas_call | solution.py:292
  46.3 2.4 %collective-permute-start.20 = (bf16[640,128]{1,0:T(8,128)(2,1)S(1)}, bf16[640,128]{1,0:T(8,128)(2,1)S(1)}, u32[]{:S(2)}, u32[]{:S(2)}) collective-permute-start(bf16[640,128]{1,0:T(8,128)(2,1)S(1)} %get-tuple-element.85.own.refs_0_), channel_id=1, source_target_pairs={{0,3},{1,0},{2,1},{3,2},{4,7},{5,4},{6,5},{7,6},{8,11},{9,8},{10,9... | collective-permute-start | bytes 491528 | tf_op jit(solution)/shard_map/ppermute | solution.py:384
  48.7 0.3 collective-permute-start.19
  49.0 0.3 collective-permute-start.18
  49.3 4.2 %collective-permute-start.23 = (bf16[640,128]{1,0:T(8,128)(2,1)S(1)}, bf16[640,128]{1,0:T(8,128)(2,1)S(1)}, u32[]{:S(2)}, u32[]{:S(2)}) collective-permute-start(bf16[640,128]{1,0:T(8,128)(2,1)S(1)} %get-tuple-element.85.own.refs_0_), channel_id=1, source_target_pairs={{0,8},{1,9},{2,10},{3,11},{4,12},{5,13},{6,14},{7,15},{8,0},{9,1},... | collective-permute-start | bytes 491528 | tf_op jit(solution)/shard_map/ppermute | solution.py:380
  53.5 0.7 collective-permute-start.22
  54.2 3.4 %collective-permute-start.21 = (bf16[640,128]{1,0:T(8,128)(2,1)S(1)}, bf16[640,128]{1,0:T(8,128)(2,1)S(1)}, u32[]{:S(2)}, u32[]{:S(2)}) collective-permute-start(bf16[640,128]{1,0:T(8,128)(2,1)S(1)} %get-tuple-element.85.own.refs_0_), channel_id=1, source_target_pairs={{0,4},{1,5},{2,6},{3,7},{4,8},{5,9},{6,10},{7,11},{8,12},{9,13},{1... | collective-permute-start | bytes 491528 | tf_op jit(solution)/shard_map/ppermute | solution.py:380
  57.7 4.2 %collective-permute-start.28 = (bf16[1664,128]{1,0:T(8,128)(2,1)S(1)}, bf16[1664,128]{1,0:T(8,128)(2,1)S(1)}, u32[]{:S(2)}, u32[]{:S(2)}) collective-permute-start(bf16[1664,128]{1,0:T(8,128)(2,1)S(1)} %merge_z.1.refs_1_.rest), channel_id=1, source_target_pairs={{0,12},{1,13},{2,14},{3,15},{4,0},{5,1},{6,2},{7,3},{8,4},{9,5},{1... | collective-permute-start | bytes 1277960 | tf_op jit(solution)/shard_map/ppermute | solution.py:380
  61.8 0.9 collective-permute-start.26
  62.8 0.2 collective-permute-start.25
  63.0 0.8 collective-permute-start.24
  63.8 4.3 %backward_early.1.before = f32[33,128,128]{2,1,0:T(8,128)S(1)} custom-call(s32[1,640]{1,0:T(1,128)S(1)} %get-tuple-element.84.codes_ref, bf16[512,128,128]{2,1,0:T(8,128)(2,1)S(1)} %get-tuple-element.58.adj_ref, bf16[640,128]{1,0:T(8,128)(2,1)S(1)} %get-tuple-element.85.own.refs_0_, bf16[1664,128]{1,0:T(8,128)(2,1)S(1)} %merge_z.1.refs_1_.rest, ...), custom_call_target="tpu_custom_call" | custom-call | flops 3221225472 | bytes 7864320 | tf_op jit(solution)/shard_map/backward_early/pallas_call | solution.py:147
  68.1 0.5 collective-permute-done.25.refs_1_
  68.5 3.9 %collective-permute-done.24.refs_0_ = bf16[640,128]{1,0:T(8,128)(2,1)S(1)} collective-permute-done((bf16[640,128]{1,0:T(8,128)(2,1)S(1)}, bf16[640,128]{1,0:T(8,128)(2,1)S(1)}, u32[]{:S(2)}, u32[]{:S(2)}) %collective-permute-start.24) | collective-permute-done | bytes 163872 | tf_op jit(solution)/shard_map/ppermute | solution.py:384
  72.5 0.2 collective-permute-done.27.refs_3_
  72.7 3.4 %backward_other.1 = (f32[2176,128]{1,0:T(8,128)S(1)}, f32[128,128]{1,0:T(8,128)S(1)}, bf16[36,128,128]{2,1,0:T(8,128)(2,1)S(1)}) custom-call(s32[1,640]{1,0:T(1,128)S(1)} %get-tuple-element.86.codes_ref, bf16[512,128,128]{2,1,0:T(8,128)(2,1)S(1)} %get-tuple-element.58.adj_ref, f32[33,128,128]{2,1,0:T(8,128)S(1)} %backward_early.1.before, ...), custom_call_target="tpu_custom_call" | custom-call | flops 2576980480 | bytes 6291456 | tf_op jit(solution)/shard_map/backward_other/pallas_call | solution.py:147
  76.1 1.8 %collective-permute-start.29 = (f32[2176,128]{1,0:T(8,128)S(1)}, f32[2176,128]{1,0:T(8,128)S(1)}, u32[]{:S(2)}, u32[]{:S(2)}) collective-permute-start(f32[2176,128]{1,0:T(8,128)S(1)} %get-tuple-element.89), channel_id=1, source_target_pairs={{0,16},{16,0},{32,48},{48,32},{64,80},{80,64},{96,112},{112,96},{1... | collective-permute-start | bytes 3342344 | tf_op jit(solution)/shard_map/ppermute | solution.py:392
  77.9 2.5 %backward_own.1.keep = f32[2048,128]{1,0:T(8,128)S(1)} custom-call(s32[1,640]{1,0:T(1,128)S(1)} %get-tuple-element.83.codes_ref, bf16[512,128,128]{2,1,0:T(8,128)(2,1)S(1)} %get-tuple-element.58.adj_ref, f32[33,128,128]{2,1,0:T(8,128)S(1)} %backward_early.1.before, bf16[36,128,128]{2,1,0:T(8,128)(2,1)S(1)} %get-tuple-element.87.slopes), custom_call_target="tpu_custom_call" | custom-call | flops 2576980480 | bytes 6291456 | tf_op jit(solution)/shard_map/backward_own/pallas_call | solution.py:147
  80.4 0.1 add_core.1
  80.5 0.2 collective-permute-start.30
  80.8 2.9 %collective-permute-start.31 = (bf16[640,128]{1,0:T(8,128)(2,1)S(1)}, bf16[640,128]{1,0:T(8,128)(2,1)S(1)}, u32[]{:S(2)}, u32[]{:S(2)}) collective-permute-start(bf16[640,128]{1,0:T(8,128)(2,1)S(1)} %get-tuple-element.93), channel_id=1, source_target_pairs={{0,64},{16,80},{32,96},{48,112},{64,0},{80,16},{96,32},{112,48},{1... | collective-permute-start | bytes 491528 | tf_op jit(solution)/shard_map/ppermute | solution.py:388
  83.7 3.6 %collective-permute-done.30.refs_0_ = bf16[640,128]{1,0:T(8,128)(2,1)S(1)} collective-permute-done((bf16[640,128]{1,0:T(8,128)(2,1)S(1)}, bf16[640,128]{1,0:T(8,128)(2,1)S(1)}, u32[]{:S(2)}, u32[]{:S(2)}) %collective-permute-start.30) | collective-permute-done | bytes 163872 | tf_op jit(solution)/shard_map/ppermute | solution.py:388
  87.3 4.3 %collective-permute-done.31.refs_1_ = bf16[640,128]{1,0:T(8,128)(2,1)S(1)} collective-permute-done((bf16[640,128]{1,0:T(8,128)(2,1)S(1)}, bf16[640,128]{1,0:T(8,128)(2,1)S(1)}, u32[]{:S(2)}, u32[]{:S(2)}) %collective-permute-start.31) | collective-permute-done | bytes 163872 | tf_op jit(solution)/shard_map/ppermute | solution.py:388
  91.6 1.0 %finish.1 = (bf16[512,128]{1,0:T(8,128)(2,1)}, f32[128,128]{1,0:T(8,128)}) custom-call(bf16[128,128]{1,0:T(8,128)(2,1)S(1)} %copy-done.2, f32[512,128]{1,0:T(8,128)S(1)} %get-tuple-element.90.own, f32[128,128]{1,0:T(8,128)S(1)} %get-tuple-element.91.wown, bf16[640,128]{1,0:T(8,128)(2,1)S(1)} %collective-permute-done.30.refs_0_, ...), custom_call_target="tpu_custom_call" | custom-call | tf_op jit(solution)/shard_map/finish/pallas_call | solution.py:366
  (22 shorter events, 0.1 us)
Async XLA Ops:
  0.6 13.4 %collective-permute-start.2 = (bf16[512,128]{1,0:T(8,128)(2,1)}, bf16[512,128]{1,0:T(8,128)(2,1)S(1)}, u32[]{:S(2)}, u32[]{:S(2)}) collective-permute-start(bf16[512,128]{1,0:T(8,128)(2,1)} %refs_0_.1), channel_id=1, source_target_pairs={{0,96},{16,112},{32,0},{48,16},{64,32},{80,48},{96,64},{112,80},{1... | collective-permute-start | bytes 393224 | tf_op jit(solution)/shard_map/ppermute | solution.py:388
  4.3 9.8 %collective-permute-start.1 = (bf16[512,128]{1,0:T(8,128)(2,1)}, bf16[512,128]{1,0:T(8,128)(2,1)S(1)}, u32[]{:S(2)}, u32[]{:S(2)}) collective-permute-start(bf16[512,128]{1,0:T(8,128)(2,1)} %refs_0_.1), channel_id=1, source_target_pairs={{0,64},{16,80},{32,96},{48,112},{64,0},{80,16},{96,32},{112,48},{1... | collective-permute-start | bytes 393224 | tf_op jit(solution)/shard_map/ppermute | solution.py:388
  4.6 9.5 %collective-permute-start = (bf16[512,128]{1,0:T(8,128)(2,1)}, bf16[512,128]{1,0:T(8,128)(2,1)S(1)}, u32[]{:S(2)}, u32[]{:S(2)}) collective-permute-start(bf16[512,128]{1,0:T(8,128)(2,1)} %refs_0_.1), channel_id=1, source_target_pairs={{0,32},{16,48},{32,64},{48,80},{64,96},{80,112},{96,0},{112,16},{1... | collective-permute-start | bytes 393224 | tf_op jit(solution)/shard_map/ppermute | solution.py:388
  5.3 9.9 %collective-permute-start.3 = (bf16[512,128]{1,0:T(8,128)(2,1)}, bf16[512,128]{1,0:T(8,128)(2,1)S(1)}, u32[]{:S(2)}, u32[]{:S(2)}) collective-permute-start(bf16[512,128]{1,0:T(8,128)(2,1)} %refs_0_.1), channel_id=1, source_target_pairs={{0,16},{16,0},{32,48},{48,32},{64,80},{80,64},{96,112},{112,96},{1... | collective-permute-start | bytes 393224 | tf_op jit(solution)/shard_map/ppermute | solution.py:392
  8.2 8.1 %copy-start = (bf16[512,128]{1,0:T(8,128)(2,1)S(1)}, bf16[512,128]{1,0:T(8,128)(2,1)}, u32[]{:S(2)}) copy-start(bf16[512,128]{1,0:T(8,128)(2,1)} %refs_0_.1) | copy-start | bytes 393220
  14.1 1.6 %collective-permute-start.4 = (bf16[512,128]{1,0:T(8,128)(2,1)S(1)}, bf16[512,128]{1,0:T(8,128)(2,1)S(1)}, u32[]{:S(2)}, u32[]{:S(2)}) collective-permute-start(bf16[512,128]{1,0:T(8,128)(2,1)S(1)} %collective-permute-done.refs_1_), channel_id=1, source_target_pairs={{0,16},{16,0},{32,48},{48,32},{64,80},{80,64},{96,112},{112,96},{1... | collective-permute-start | bytes 393224 | tf_op jit(solution)/shard_map/ppermute | solution.py:392
  14.7 1.3 %collective-permute-start.5 = (bf16[512,128]{1,0:T(8,128)(2,1)S(1)}, bf16[512,128]{1,0:T(8,128)(2,1)S(1)}, u32[]{:S(2)}, u32[]{:S(2)}) collective-permute-start(bf16[512,128]{1,0:T(8,128)(2,1)S(1)} %collective-permute-done.1.refs_2_), channel_id=1, source_target_pairs={{0,16},{16,0},{32,48},{48,32},{64,80},{80,64},{96,112},{112,96},{1... | collective-permute-start | bytes 393224 | tf_op jit(solution)/shard_map/ppermute | solution.py:392
  14.7 1.5 %collective-permute-start.6 = (bf16[512,128]{1,0:T(8,128)(2,1)S(1)}, bf16[512,128]{1,0:T(8,128)(2,1)S(1)}, u32[]{:S(2)}, u32[]{:S(2)}) collective-permute-start(bf16[512,128]{1,0:T(8,128)(2,1)S(1)} %collective-permute-done.2.refs_3_), channel_id=1, source_target_pairs={{0,16},{16,0},{32,48},{48,32},{64,80},{80,64},{96,112},{112,96},{1... | collective-permute-start | bytes 393224 | tf_op jit(solution)/shard_map/ppermute | solution.py:392
  19.7 14.8 %collective-permute-start.7 = (bf16[1536,128]{1,0:T(8,128)(2,1)S(1)}, bf16[1536,128]{1,0:T(8,128)(2,1)S(1)}, u32[]{:S(2)}, u32[]{:S(2)}) collective-permute-start(bf16[1536,128]{1,0:T(8,128)(2,1)S(1)} %get-tuple-element.68), channel_id=1, source_target_pairs={{0,4},{1,5},{2,6},{3,7},{4,8},{5,9},{6,10},{7,11},{8,12},{9,13},{1... | collective-permute-start | bytes 1179656 | tf_op jit(solution)/shard_map/ppermute | solution.py:380
  20.1 14.5 %collective-permute-start.8 = (bf16[1536,128]{1,0:T(8,128)(2,1)S(1)}, bf16[1536,128]{1,0:T(8,128)(2,1)S(1)}, u32[]{:S(2)}, u32[]{:S(2)}) collective-permute-start(bf16[1536,128]{1,0:T(8,128)(2,1)S(1)} %get-tuple-element.69), channel_id=1, source_target_pairs={{0,12},{1,13},{2,14},{3,15},{4,0},{5,1},{6,2},{7,3},{8,4},{9,5},{1... | collective-permute-start | bytes 1179656 | tf_op jit(solution)/shard_map/ppermute | solution.py:380
  25.1 10.1 %collective-permute-start.14 = (bf16[512,128]{1,0:T(8,128)(2,1)S(1)}, bf16[512,128]{1,0:T(8,128)(2,1)S(1)}, u32[]{:S(2)}, u32[]{:S(2)}) collective-permute-start(bf16[512,128]{1,0:T(8,128)(2,1)S(1)} %get-tuple-element.79), channel_id=1, source_target_pairs={{0,1},{1,2},{2,3},{3,0},{4,5},{5,6},{6,7},{7,4},{8,9},{9,10},{10,1... | collective-permute-start | bytes 393224 | tf_op jit(solution)/shard_map/ppermute | solution.py:384
  26.8 11.1 %collective-permute-start.15 = (bf16[512,128]{1,0:T(8,128)(2,1)S(1)}, bf16[512,128]{1,0:T(8,128)(2,1)S(1)}, u32[]{:S(2)}, u32[]{:S(2)}) collective-permute-start(bf16[512,128]{1,0:T(8,128)(2,1)S(1)} %get-tuple-element.80), channel_id=1, source_target_pairs={{0,2},{1,3},{2,0},{3,1},{4,6},{5,7},{6,4},{7,5},{8,10},{9,11},{10,... | collective-permute-start | bytes 393224 | tf_op jit(solution)/shard_map/ppermute | solution.py:384
  30.1 7.8 %collective-permute-start.16 = (bf16[512,128]{1,0:T(8,128)(2,1)S(1)}, bf16[512,128]{1,0:T(8,128)(2,1)S(1)}, u32[]{:S(2)}, u32[]{:S(2)}) collective-permute-start(bf16[512,128]{1,0:T(8,128)(2,1)S(1)} %get-tuple-element.81), channel_id=1, source_target_pairs={{0,3},{1,0},{2,1},{3,2},{4,7},{5,4},{6,5},{7,6},{8,11},{9,8},{10,9... | collective-permute-start | bytes 393224 | tf_op jit(solution)/shard_map/ppermute | solution.py:384
  34.5 10.8 %copy-start.1 = (bf16[512,128]{1,0:T(8,128)(2,1)S(1)}, bf16[512,128]{1,0:T(8,128)(2,1)}, u32[]{:S(2)}) copy-start(bf16[512,128]{1,0:T(8,128)(2,1)} %grad_ref.1) | copy-start | bytes 393220
  34.5 10.8 %copy-start.2 = (bf16[128,128]{1,0:T(8,128)(2,1)S(1)}, bf16[128,128]{1,0:T(8,128)(2,1)}, u32[]{:S(2)}) copy-start(bf16[128,128]{1,0:T(8,128)(2,1)} %weight_ref.3) | copy-start | bytes 98308
  34.7 6.4 %collective-permute-start.9 = (bf16[512,128]{1,0:T(8,128)(2,1)S(1)}, bf16[512,128]{1,0:T(8,128)(2,1)S(1)}, u32[]{:S(2)}, u32[]{:S(2)}) collective-permute-start(bf16[512,128]{1,0:T(8,128)(2,1)S(1)} %get-tuple-element.73), channel_id=1, source_target_pairs={{0,1},{1,2},{2,3},{3,0},{4,5},{5,6},{6,7},{7,4},{8,9},{9,10},{10,1... | collective-permute-start | bytes 393224 | tf_op jit(solution)/shard_map/ppermute | solution.py:384
  35.2 6.6 %collective-permute-start.12 = (bf16[512,128]{1,0:T(8,128)(2,1)S(1)}, bf16[512,128]{1,0:T(8,128)(2,1)S(1)}, u32[]{:S(2)}, u32[]{:S(2)}) collective-permute-start(bf16[512,128]{1,0:T(8,128)(2,1)S(1)} %get-tuple-element.76), channel_id=1, source_target_pairs={{0,4},{1,5},{2,6},{3,7},{4,8},{5,9},{6,10},{7,11},{8,12},{9,13},{1... | collective-permute-start | bytes 393224 | tf_op jit(solution)/shard_map/ppermute | solution.py:380
  35.2 6.6 %collective-permute-start.13 = (bf16[512,128]{1,0:T(8,128)(2,1)S(1)}, bf16[512,128]{1,0:T(8,128)(2,1)S(1)}, u32[]{:S(2)}, u32[]{:S(2)}) collective-permute-start(bf16[512,128]{1,0:T(8,128)(2,1)S(1)} %get-tuple-element.77), channel_id=1, source_target_pairs={{0,12},{1,13},{2,14},{3,15},{4,0},{5,1},{6,2},{7,3},{8,4},{9,5},{1... | collective-permute-start | bytes 393224 | tf_op jit(solution)/shard_map/ppermute | solution.py:380
  38.0 5.6 %collective-permute-start.17 = (bf16[512,128]{1,0:T(8,128)(2,1)S(1)}, bf16[512,128]{1,0:T(8,128)(2,1)S(1)}, u32[]{:S(2)}, u32[]{:S(2)}) collective-permute-start(bf16[512,128]{1,0:T(8,128)(2,1)S(1)} %add_z.1), channel_id=1, source_target_pairs={{0,8},{1,9},{2,10},{3,11},{4,12},{5,13},{6,14},{7,15},{8,0},{9,1},... | collective-permute-start | bytes 393224 | tf_op jit(solution)/shard_map/ppermute | solution.py:380
  38.1 5.5 %collective-permute-start.10 = (bf16[512,128]{1,0:T(8,128)(2,1)S(1)}, bf16[512,128]{1,0:T(8,128)(2,1)S(1)}, u32[]{:S(2)}, u32[]{:S(2)}) collective-permute-start(bf16[512,128]{1,0:T(8,128)(2,1)S(1)} %get-tuple-element.74), channel_id=1, source_target_pairs={{0,2},{1,3},{2,0},{3,1},{4,6},{5,7},{6,4},{7,5},{8,10},{9,11},{10,... | collective-permute-start | bytes 393224 | tf_op jit(solution)/shard_map/ppermute | solution.py:384
  41.1 4.2 %collective-permute-start.11 = (bf16[512,128]{1,0:T(8,128)(2,1)S(1)}, bf16[512,128]{1,0:T(8,128)(2,1)S(1)}, u32[]{:S(2)}, u32[]{:S(2)}) collective-permute-start(bf16[512,128]{1,0:T(8,128)(2,1)S(1)} %get-tuple-element.75), channel_id=1, source_target_pairs={{0,3},{1,0},{2,1},{3,2},{4,7},{5,4},{6,5},{7,6},{8,11},{9,8},{10,9... | collective-permute-start | bytes 393224 | tf_op jit(solution)/shard_map/ppermute | solution.py:384
  46.3 7.9 %collective-permute-start.20 = (bf16[640,128]{1,0:T(8,128)(2,1)S(1)}, bf16[640,128]{1,0:T(8,128)(2,1)S(1)}, u32[]{:S(2)}, u32[]{:S(2)}) collective-permute-start(bf16[640,128]{1,0:T(8,128)(2,1)S(1)} %get-tuple-element.85.own.refs_0_), channel_id=1, source_target_pairs={{0,3},{1,0},{2,1},{3,2},{4,7},{5,4},{6,5},{7,6},{8,11},{9,8},{10,9... | collective-permute-start | bytes 491528 | tf_op jit(solution)/shard_map/ppermute | solution.py:384
  48.7 8.9 %collective-permute-start.19 = (bf16[640,128]{1,0:T(8,128)(2,1)S(1)}, bf16[640,128]{1,0:T(8,128)(2,1)S(1)}, u32[]{:S(2)}, u32[]{:S(2)}) collective-permute-start(bf16[640,128]{1,0:T(8,128)(2,1)S(1)} %get-tuple-element.85.own.refs_0_), channel_id=1, source_target_pairs={{0,2},{1,3},{2,0},{3,1},{4,6},{5,7},{6,4},{7,5},{8,10},{9,11},{10,... | collective-permute-start | bytes 491528 | tf_op jit(solution)/shard_map/ppermute | solution.py:384
  49.0 8.6 %collective-permute-start.18 = (bf16[640,128]{1,0:T(8,128)(2,1)S(1)}, bf16[640,128]{1,0:T(8,128)(2,1)S(1)}, u32[]{:S(2)}, u32[]{:S(2)}) collective-permute-start(bf16[640,128]{1,0:T(8,128)(2,1)S(1)} %get-tuple-element.85.own.refs_0_), channel_id=1, source_target_pairs={{0,1},{1,2},{2,3},{3,0},{4,5},{5,6},{6,7},{7,4},{8,9},{9,10},{10,1... | collective-permute-start | bytes 491528 | tf_op jit(solution)/shard_map/ppermute | solution.py:384
  49.3 12.6 %collective-permute-start.23 = (bf16[640,128]{1,0:T(8,128)(2,1)S(1)}, bf16[640,128]{1,0:T(8,128)(2,1)S(1)}, u32[]{:S(2)}, u32[]{:S(2)}) collective-permute-start(bf16[640,128]{1,0:T(8,128)(2,1)S(1)} %get-tuple-element.85.own.refs_0_), channel_id=1, source_target_pairs={{0,8},{1,9},{2,10},{3,11},{4,12},{5,13},{6,14},{7,15},{8,0},{9,1},... | collective-permute-start | bytes 491528 | tf_op jit(solution)/shard_map/ppermute | solution.py:380
  53.5 9.3 %collective-permute-start.22 = (bf16[640,128]{1,0:T(8,128)(2,1)S(1)}, bf16[640,128]{1,0:T(8,128)(2,1)S(1)}, u32[]{:S(2)}, u32[]{:S(2)}) collective-permute-start(bf16[640,128]{1,0:T(8,128)(2,1)S(1)} %get-tuple-element.85.own.refs_0_), channel_id=1, source_target_pairs={{0,12},{1,13},{2,14},{3,15},{4,0},{5,1},{6,2},{7,3},{8,4},{9,5},{1... | collective-permute-start | bytes 491528 | tf_op jit(solution)/shard_map/ppermute | solution.py:380
  54.2 8.8 %collective-permute-start.21 = (bf16[640,128]{1,0:T(8,128)(2,1)S(1)}, bf16[640,128]{1,0:T(8,128)(2,1)S(1)}, u32[]{:S(2)}, u32[]{:S(2)}) collective-permute-start(bf16[640,128]{1,0:T(8,128)(2,1)S(1)} %get-tuple-element.85.own.refs_0_), channel_id=1, source_target_pairs={{0,4},{1,5},{2,6},{3,7},{4,8},{5,9},{6,10},{7,11},{8,12},{9,13},{1... | collective-permute-start | bytes 491528 | tf_op jit(solution)/shard_map/ppermute | solution.py:380
  57.7 14.8 %collective-permute-start.28 = (bf16[1664,128]{1,0:T(8,128)(2,1)S(1)}, bf16[1664,128]{1,0:T(8,128)(2,1)S(1)}, u32[]{:S(2)}, u32[]{:S(2)}) collective-permute-start(bf16[1664,128]{1,0:T(8,128)(2,1)S(1)} %merge_z.1.refs_1_.rest), channel_id=1, source_target_pairs={{0,12},{1,13},{2,14},{3,15},{4,0},{5,1},{6,2},{7,3},{8,4},{9,5},{1... | collective-permute-start | bytes 1277960 | tf_op jit(solution)/shard_map/ppermute | solution.py:380
  61.8 10.8 %collective-permute-start.27 = (bf16[1664,128]{1,0:T(8,128)(2,1)S(1)}, bf16[1664,128]{1,0:T(8,128)(2,1)S(1)}, u32[]{:S(2)}, u32[]{:S(2)}) collective-permute-start(bf16[1664,128]{1,0:T(8,128)(2,1)S(1)} %merge_z.1.refs_1_.rest), channel_id=1, source_target_pairs={{0,4},{1,5},{2,6},{3,7},{4,8},{5,9},{6,10},{7,11},{8,12},{9,13},{1... | collective-permute-start | bytes 1277960 | tf_op jit(solution)/shard_map/ppermute | solution.py:380
  61.8 6.2 %collective-permute-start.26 = (bf16[640,128]{1,0:T(8,128)(2,1)S(1)}, bf16[640,128]{1,0:T(8,128)(2,1)S(1)}, u32[]{:S(2)}, u32[]{:S(2)}) collective-permute-start(bf16[640,128]{1,0:T(8,128)(2,1)S(1)} %collective-permute-done.23.refs_4_.level), channel_id=1, source_target_pairs={{0,3},{1,0},{2,1},{3,2},{4,7},{5,4},{6,5},{7,6},{8,11},{9,8},{10,9... | collective-permute-start | bytes 491528 | tf_op jit(solution)/shard_map/ppermute | solution.py:384
  62.8 5.8 %collective-permute-start.25 = (bf16[640,128]{1,0:T(8,128)(2,1)S(1)}, bf16[640,128]{1,0:T(8,128)(2,1)S(1)}, u32[]{:S(2)}, u32[]{:S(2)}) collective-permute-start(bf16[640,128]{1,0:T(8,128)(2,1)S(1)} %collective-permute-done.23.refs_4_.level), channel_id=1, source_target_pairs={{0,2},{1,3},{2,0},{3,1},{4,6},{5,7},{6,4},{7,5},{8,10},{9,11},{10,... | collective-permute-start | bytes 491528 | tf_op jit(solution)/shard_map/ppermute | solution.py:384
  63.0 9.4 %collective-permute-start.24 = (bf16[640,128]{1,0:T(8,128)(2,1)S(1)}, bf16[640,128]{1,0:T(8,128)(2,1)S(1)}, u32[]{:S(2)}, u32[]{:S(2)}) collective-permute-start(bf16[640,128]{1,0:T(8,128)(2,1)S(1)} %collective-permute-done.23.refs_4_.level), channel_id=1, source_target_pairs={{0,1},{1,2},{2,3},{3,0},{4,5},{5,6},{6,7},{7,4},{8,9},{9,10},{10,1... | collective-permute-start | bytes 491528 | tf_op jit(solution)/shard_map/ppermute | solution.py:384
  76.1 4.3 %collective-permute-start.29 = (f32[2176,128]{1,0:T(8,128)S(1)}, f32[2176,128]{1,0:T(8,128)S(1)}, u32[]{:S(2)}, u32[]{:S(2)}) collective-permute-start(f32[2176,128]{1,0:T(8,128)S(1)} %get-tuple-element.89), channel_id=1, source_target_pairs={{0,16},{16,0},{32,48},{48,32},{64,80},{80,64},{96,112},{112,96},{1... | collective-permute-start | bytes 3342344 | tf_op jit(solution)/shard_map/ppermute | solution.py:392
  80.5 6.8 %collective-permute-start.30 = (bf16[640,128]{1,0:T(8,128)(2,1)S(1)}, bf16[640,128]{1,0:T(8,128)(2,1)S(1)}, u32[]{:S(2)}, u32[]{:S(2)}) collective-permute-start(bf16[640,128]{1,0:T(8,128)(2,1)S(1)} %get-tuple-element.92), channel_id=1, source_target_pairs={{0,32},{16,48},{32,64},{48,80},{64,96},{80,112},{96,0},{112,16},{1... | collective-permute-start | bytes 491528 | tf_op jit(solution)/shard_map/ppermute | solution.py:388
  80.8 10.9 %collective-permute-start.31 = (bf16[640,128]{1,0:T(8,128)(2,1)S(1)}, bf16[640,128]{1,0:T(8,128)(2,1)S(1)}, u32[]{:S(2)}, u32[]{:S(2)}) collective-permute-start(bf16[640,128]{1,0:T(8,128)(2,1)S(1)} %get-tuple-element.93), channel_id=1, source_target_pairs={{0,64},{16,80},{32,96},{48,112},{64,0},{80,16},{96,32},{112,48},{1... | collective-permute-start | bytes 491528 | tf_op jit(solution)/shard_map/ppermute | solution.py:388
  83.7 8.0 %collective-permute-start.32 = (bf16[640,128]{1,0:T(8,128)(2,1)S(1)}, bf16[640,128]{1,0:T(8,128)(2,1)S(1)}, u32[]{:S(2)}, u32[]{:S(2)}) collective-permute-start(bf16[640,128]{1,0:T(8,128)(2,1)S(1)} %get-tuple-element.94), channel_id=1, source_target_pairs={{0,96},{16,112},{32,0},{48,16},{64,32},{80,48},{96,64},{112,80},{1... | collective-permute-start | bytes 491528 | tf_op jit(solution)/shard_map/ppermute | solution.py:388
where the time goes:
time: 92.7 us; the launch traced here: 92.6 us
  starting transfers between devices  44.7 us (48%)
  Pallas kernels  28.7 us (31%)
  waiting for transfers between devices  17.1 us (18%)
  between operations  1.45 us (2%)
    pallas_call x6, Pallas kernels, sparse_call(): pl.pallas_call(kernel, out_shape=[jax.ShapeDtypeStruct(shape, dtype) for...  20.5 us
    ppermute x10, starting transfers between devices, shift_x(): lax.ppermute(a, 'col', [(i, (i // NZ + d) % NX * NZ + i % NZ) for i in ra...  18 us
    ppermute x12, starting transfers between devices, shift_z(): lax.ppermute(a, 'col', [(i, i // NZ * NZ + (i % NZ + d) % NZ) for i in ra...  14.4 us
    ppermute x6, waiting for transfers between devices, shift_y(): lax.ppermute(a, 'row', [(i, (i // 2 + d) % NY * 2 + i % 2) for i in range...  8.03 us
    ppermute x6, starting transfers between devices, shift_y(): lax.ppermute(a, 'row', [(i, (i // 2 + d) % NY * 2 + i % 2) for i in range...  7.83 us
    ppermute x12, waiting for transfers between devices, shift_z(): lax.ppermute(a, 'col', [(i, i // NZ * NZ + (i % NZ + d) % NZ) for i in ra...  6.11 us
    pallas_call x1, Pallas kernels, prepare(): pl.pallas_call(prepare_kernel, out_shape=[jax.ShapeDtypeStruct(adjacency....  5.82 us
    ppermute x5, starting transfers between devices, swap_core(): return lax.ppermute(a, 'row', [(i, i ^ 1) for i in range(NY * 2)])  4.44 us
  transfers between devices with their start and end apart: 33, of which 11 were waited for; matrix products, arithmetic and copies ran while one was open for 1% of the time, Pallas kernels for 21%

commit v1 on v0

--- a/solution.py
+++ b/solution.py
@@ -192,7 +192,7 @@
 def gather_slopes(slopes, ins):
     at = 0
     for part in ins:
-        blocks = part.shape[0] // BLK - 1
+        blocks = part.shape[0] // BLK // OWN * OWN
         slopes[pl.ds(at, blocks)] = part[pl.ds(0, blocks * BLK)].reshape(blocks, BLK, BLK)
         at += blocks
 
@@ -262,7 +262,7 @@
 
 
 def activate_kernel(weight_ref, grad_ref, *refs):
-    parts, (act_ref, pay_ref) = refs[:-2], refs[-2:]
+    parts, (act_ref, slope_ref, pay_ref) = refs[:-3], refs[-3:]
     rows = act_ref.shape[0]
     total = parts[0][...]
     for part in parts[1:]:
@@ -281,6 +281,7 @@
     wterm = jnp.zeros((BLK, BLK), F32)
     for b in range(0, rows, BLK):
         turned = slope[b : b + BLK].T
+        slope_ref[pl.ds(b, BLK)] = turned
         pay_ref[pl.ds(b, BLK)] = turned
         wterm += jnp.dot(turned, high[b : b + BLK], preferred_element_type=F32)
         wterm += jnp.dot(turned, low[b : b + BLK], preferred_element_type=F32)
@@ -293,10 +294,11 @@
         activate_kernel,
         out_shape=[
             jax.ShapeDtypeStruct((rows, BLK), BF16),
+            jax.ShapeDtypeStruct((rows, BLK), BF16),
             jax.ShapeDtypeStruct((rows + BLK, BLK), BF16),
         ],
         in_specs=vmem_specs(2 + len(parts)),
-        out_specs=vmem_specs(2),
+        out_specs=vmem_specs(3),
         compiler_params=params(),
         name="activate",
     )(weight, grad_out, *parts)
@@ -441,11 +443,11 @@
     z1, z2, z3 = shift_z(z1, 1), shift_z(z2, 2), shift_z(z3, 3)
     across = add_split([across] + from_z, [BF16], "add_z")[0]
     parts = [own, z1, z2, z3, shift_x(n1, 1), shift_x(n3, 3), shift_x(across, 2)]
-    activated, pay = activate(weight, grad_out, parts)
+    activated, slope, pay = activate(weight, grad_out, parts)
 
     beside = [shift_z(pay, d) for d in range(1, NZ)]
     across = shift_x(pay, 2)
-    n1, n3 = shift_x(pay, 1), shift_x(pay, 3)
+    n1, n3 = shift_x(slope, 1), shift_x(slope, 3)
     rest = merge(pay, beside)
     first, second = shift_x(rest, 1), shift_x(rest, 3)
     across = [across] + [shift_z(across, d) for d in range(1, NZ)]
@@ -483,7 +485,7 @@
         "backward_own",
     )[0]
     *parts, own, wown = add_core(keep, wkeep, got)
-    parts = [shift_y(part, d) for d, part in enumerate(parts, 1)]
+    parts = [shift_y(parts[d - 1], d) for d in (2, 1, 3)]
     nodes_all = own_rows * lax.axis_size("row") * lax.axis_size("col")
     input_grad, weight_grad = finish(nodes_all ** (-0.5), weight, own, wown, parts)
     return (activated, input_grad, weight_grad)

time: 92.7 us -> 92.4 us (level)
  waiting for transfers between devices: 17.1 us -> 22.4 us
  starting transfers between devices: 44.7 us -> 40.8 us
  Pallas kernels: 28.7 us -> 26.1 us
    ppermute x12, waiting for transfers between devices: 6.11 us -> 14.5 us  [shift_z(): lax.ppermute(a, 'col', [(i, i // NZ * NZ + (i % NZ + d) % NZ) for i in ra...]
    ppermute x10, starting transfers between devices: 18 us -> 10.2 us  [shift_x(): lax.ppermute(a, 'col', [(i, (i // NZ + d) % NX * NZ + i % NZ) for i in ra...]
    pallas_call x6, Pallas kernels: 20.5 us -> 17.9 us  [sparse_call(): pl.pallas_call(kernel, out_shape=[jax.ShapeDtypeStruct(shape, dtype) for...]
    ppermute x6, starting transfers between devices: 7.83 us -> 9.96 us  [shift_y(): lax.ppermute(a, 'row', [(i, (i // 2 + d) % NY * 2 + i % 2) for i in range...]
    ppermute x6, waiting for transfers between devices: 8.03 us -> 6 us  [shift_y(): lax.ppermute(a, 'row', [(i, (i // 2 + d) % NY * 2 + i % 2) for i in range...]
    ppermute x5, starting transfers between devices: 4.44 us -> 5.59 us  [swap_core(): return lax.ppermute(a, 'row', [(i, i ^ 1) for i in range(NY * 2)])]
    ppermute x10, waiting for transfers between devices: 1.95 us -> 0.81 us  [shift_x(): lax.ppermute(a, 'col', [(i, (i // NZ + d) % NX * NZ + i % NZ) for i in ra...]
  transfers between devices with their start and end apart: 33 -> 33, of which waited for: 11 -> 13; matrix products, arithmetic and copies ran while one was open for 1% -> 1% of each run, Pallas kernels for 21% -> 20%
where the time goes in v1:
time: 92.4 us; the launch traced here: 91.5 us
  starting transfers between devices  40.8 us (44%)
  Pallas kernels  26.1 us (28%)
  waiting for transfers between devices  22.4 us (24%)
  between operations  1.47 us (2%)
    pallas_call x6, Pallas kernels, sparse_call(): pl.pallas_call(kernel, out_shape=[jax.ShapeDtypeStruct(shape, dtype) for...  17.9 us
    ppermute x12, starting transfers between devices, shift_z(): lax.ppermute(a, 'col', [(i, i // NZ * NZ + (i % NZ + d) % NZ) for i in ra...  15 us
    ppermute x12, waiting for transfers between devices, shift_z(): lax.ppermute(a, 'col', [(i, i // NZ * NZ + (i % NZ + d) % NZ) for i in ra...  14.5 us
    ppermute x10, starting transfers between devices, shift_x(): lax.ppermute(a, 'col', [(i, (i // NZ + d) % NX * NZ + i % NZ) for i in ra...  10.2 us
    ppermute x6, starting transfers between devices, shift_y(): lax.ppermute(a, 'row', [(i, (i // 2 + d) % NY * 2 + i % 2) for i in range...  9.96 us
    ppermute x6, waiting for transfers between devices, shift_y(): lax.ppermute(a, 'row', [(i, (i // 2 + d) % NY * 2 + i % 2) for i in range...  6 us
    pallas_call x1, Pallas kernels, prepare(): pl.pallas_call(prepare_kernel, out_shape=[jax.ShapeDtypeStruct(adjacency....  5.82 us
    ppermute x5, starting transfers between devices, swap_core(): return lax.ppermute(a, 'row', [(i, i ^ 1) for i in range(NY * 2)])  5.59 us
  transfers between devices with their start and end apart: 33, of which 13 were waited for; matrix products, arithmetic and copies ran while one was open for 1% of the time, Pallas kernels for 20%

profile of v1, /device:TPU:1, one launch (start us, length us, event | category | flops | bytes accessed | tf_op | source)
XLA Modules:
  0.0 91.5 jit_solution(1229255069141926576)
XLA Ops:
  0.6 3.6 %collective-permute-start.2 = (bf16[512,128]{1,0:T(8,128)(2,1)}, bf16[512,128]{1,0:T(8,128)(2,1)S(1)}, u32[]{:S(2)}, u32[]{:S(2)}) collective-permute-start(bf16[512,128]{1,0:T(8,128)(2,1)} %refs_0_.1), channel_id=1, source_target_pairs={{0,96},{16,112},{32,0},{48,16},{64,32},{80,48},{96,64},{112,80},{1... | collective-permute-start | bytes 393224 | tf_op jit(solution)/shard_map/ppermute | solution.py:390
  4.3 0.3 collective-permute-start.1
  4.6 0.7 collective-permute-start
  5.3 1.5 %collective-permute-start.3 = (bf16[512,128]{1,0:T(8,128)(2,1)}, bf16[512,128]{1,0:T(8,128)(2,1)S(1)}, u32[]{:S(2)}, u32[]{:S(2)}) collective-permute-start(bf16[512,128]{1,0:T(8,128)(2,1)} %refs_0_.1), channel_id=1, source_target_pairs={{0,16},{16,0},{32,48},{48,32},{64,80},{80,64},{96,112},{112,96},{1... | collective-permute-start | bytes 393224 | tf_op jit(solution)/shard_map/ppermute | solution.py:394
  7.5 0.7 compare_select_fusion.packed_ref
  8.2 5.8 %prepare.1 = (bf16[512,128,128]{2,1,0:T(8,128)(2,1)S(1)}, s32[1,640]{1,0:T(1,128)S(1)}, s32[1,640]{1,0:T(1,128)S(1)}, s32[1,640]{1,0:T(1,128)S(1)}, s32[1,640]{1...) custom-call(s32[1,512]{1,0:T(1,128)S(1)} %compare_select_fusion.packed_ref, bf16[512,128,128]{2,1,0:T(8,128)(2,1)} %bitcast.5), custom_call_target="tpu_custom_call" | custom-call | bytes 33554432 | tf_op jit(solution)/shard_map/prepare/pallas_call | solution.py:116
  14.0 0.0 collective-permute-done.1.refs_2_
  14.0 0.1 collective-permute-done.refs_1_
  14.1 0.6 collective-permute-start.4
  14.7 0.0 collective-permute-start.5
  14.7 0.5 collective-permute-start.6
  15.2 0.0 collective-permute-done.3.refs_4_
  15.2 0.5 collective-permute-done.4.refs_5_
  15.7 0.4 collective-permute-done.5.refs_6_
  16.0 0.2 collective-permute-done.6.refs_7_
  16.2 3.5 %forward_far.1 = (bf16[32,128,128]{2,1,0:T(8,128)(2,1)S(1)}, bf16[1536,128]{1,0:T(8,128)(2,1)S(1)}, bf16[1536,128]{1,0:T(8,128)(2,1)S(1)}) custom-call(s32[1,640]{1,0:T(1,128)S(1)} %get-tuple-element.60.codes_ref, bf16[512,128,128]{2,1,0:T(8,128)(2,1)S(1)} %get-tuple-element.59.adj_ref, bf16[512,128]{1,0:T(8,128)(2,1)S(1)} %copy-done, ...), custom_call_target="tpu_custom_call" | custom-call | flops 3221225472 | bytes 7864320 | tf_op jit(solution)/shard_map/forward_far/pallas_call | solution.py:147
  19.7 0.4 collective-permute-start.7
  20.1 2.4 %collective-permute-start.8 = (bf16[1536,128]{1,0:T(8,128)(2,1)S(1)}, bf16[1536,128]{1,0:T(8,128)(2,1)S(1)}, u32[]{:S(2)}, u32[]{:S(2)}) collective-permute-start(bf16[1536,128]{1,0:T(8,128)(2,1)S(1)} %get-tuple-element.70), channel_id=1, source_target_pairs={{0,12},{1,13},{2,14},{3,15},{4,0},{5,1},{6,2},{7,3},{8,4},{9,5},{1... | collective-permute-start | bytes 1179656 | tf_op jit(solution)/shard_map/ppermute | solution.py:382
  22.5 2.6 %forward_two.1 = (f32[512,128]{1,0:T(8,128)S(1)}, bf16[512,128]{1,0:T(8,128)(2,1)S(1)}, bf16[512,128]{1,0:T(8,128)(2,1)S(1)}, bf16[512,128]{1,0:T(8,128)(2,1)S(1)}) custom-call(s32[1,640]{1,0:T(1,128)S(1)} %get-tuple-element.66.codes_ref, bf16[512,128,128]{2,1,0:T(8,128)(2,1)S(1)} %get-tuple-element.59.adj_ref, bf16[32,128,128]{2,1,0:T(8,128)(2,1)S(1)} %get-tuple-element.64.feats), custom_call_target="tpu_custom_call" | custom-call | flops 2147483648 | bytes 5242880 | tf_op jit(solution)/shard_map/forward_two/pallas_call | solution.py:147
  25.1 1.1 %collective-permute-start.14 = (bf16[512,128]{1,0:T(8,128)(2,1)S(1)}, bf16[512,128]{1,0:T(8,128)(2,1)S(1)}, u32[]{:S(2)}, u32[]{:S(2)}) collective-permute-start(bf16[512,128]{1,0:T(8,128)(2,1)S(1)} %get-tuple-element.80), channel_id=1, source_target_pairs={{0,1},{1,2},{2,3},{3,0},{4,5},{5,6},{6,7},{7,4},{8,9},{9,10},{10,1... | collective-permute-start | bytes 393224 | tf_op jit(solution)/shard_map/ppermute | solution.py:386
  26.2 2.8 %collective-permute-start.15 = (bf16[512,128]{1,0:T(8,128)(2,1)S(1)}, bf16[512,128]{1,0:T(8,128)(2,1)S(1)}, u32[]{:S(2)}, u32[]{:S(2)}) collective-permute-start(bf16[512,128]{1,0:T(8,128)(2,1)S(1)} %get-tuple-element.81), channel_id=1, source_target_pairs={{0,2},{1,3},{2,0},{3,1},{4,6},{5,7},{6,4},{7,5},{8,10},{9,11},{10,... | collective-permute-start | bytes 393224 | tf_op jit(solution)/shard_map/ppermute | solution.py:386
  29.0 0.7 collective-permute-start.16
  29.8 3.4 %forward_rest.1 = (f32[512,128]{1,0:T(8,128)S(1)}, f32[1536,128]{1,0:T(8,128)S(1)}, bf16[512,128]{1,0:T(8,128)(2,1)S(1)}, bf16[512,128]{1,0:T(8,128)(2,1)S(1)}) custom-call(s32[1,640]{1,0:T(1,128)S(1)} %get-tuple-element.58.codes_ref, bf16[512,128,128]{2,1,0:T(8,128)(2,1)S(1)} %get-tuple-element.59.adj_ref, bf16[32,128,128]{2,1,0:T(8,128)(2,1)S(1)} %get-tuple-element.64.feats), custom_call_target="tpu_custom_call" | custom-call | flops 3221225472 | bytes 7864320 | tf_op jit(solution)/shard_map/forward_rest/pallas_call | solution.py:147
  33.1 0.0 copy-start.1
  33.2 0.0 copy-start.2
  33.2 0.0 collective-permute-done.7.refs_1_
  33.2 0.0 collective-permute-done.8.refs_2_
  33.2 0.1 add_x.1
  33.3 0.1 collective-permute-start.9
  33.4 0.7 collective-permute-start.12
  34.1 0.0 collective-permute-done.14.refs_1_
  34.1 2.1 %collective-permute-start.13 = (bf16[512,128]{1,0:T(8,128)(2,1)S(1)}, bf16[512,128]{1,0:T(8,128)(2,1)S(1)}, u32[]{:S(2)}, u32[]{:S(2)}) collective-permute-start(bf16[512,128]{1,0:T(8,128)(2,1)S(1)} %get-tuple-element.78), channel_id=1, source_target_pairs={{0,12},{1,13},{2,14},{3,15},{4,0},{5,1},{6,2},{7,3},{8,4},{9,5},{1... | collective-permute-start | bytes 393224 | tf_op jit(solution)/shard_map/ppermute | solution.py:382
  36.2 0.0 collective-permute-done.15.refs_2_
  36.2 0.1 add_z.1
  36.2 1.6 %collective-permute-start.17 = (bf16[512,128]{1,0:T(8,128)(2,1)S(1)}, bf16[512,128]{1,0:T(8,128)(2,1)S(1)}, u32[]{:S(2)}, u32[]{:S(2)}) collective-permute-start(bf16[512,128]{1,0:T(8,128)(2,1)S(1)} %add_z.1), channel_id=1, source_target_pairs={{0,8},{1,9},{2,10},{3,11},{4,12},{5,13},{6,14},{7,15},{8,0},{9,1},... | collective-permute-start | bytes 393224 | tf_op jit(solution)/shard_map/ppermute | solution.py:382
  37.9 2.6 %collective-permute-start.10 = (bf16[512,128]{1,0:T(8,128)(2,1)S(1)}, bf16[512,128]{1,0:T(8,128)(2,1)S(1)}, u32[]{:S(2)}, u32[]{:S(2)}) collective-permute-start(bf16[512,128]{1,0:T(8,128)(2,1)S(1)} %get-tuple-element.75), channel_id=1, source_target_pairs={{0,2},{1,3},{2,0},{3,1},{4,6},{5,7},{6,4},{7,5},{8,10},{9,11},{10,... | collective-permute-start | bytes 393224 | tf_op jit(solution)/shard_map/ppermute | solution.py:386
  40.4 1.4 %collective-permute-start.11 = (bf16[512,128]{1,0:T(8,128)(2,1)S(1)}, bf16[512,128]{1,0:T(8,128)(2,1)S(1)}, u32[]{:S(2)}, u32[]{:S(2)}) collective-permute-start(bf16[512,128]{1,0:T(8,128)(2,1)S(1)} %get-tuple-element.76), channel_id=1, source_target_pairs={{0,3},{1,0},{2,1},{3,2},{4,7},{5,4},{6,5},{7,6},{8,11},{9,8},{10,9... | collective-permute-start | bytes 393224 | tf_op jit(solution)/shard_map/ppermute | solution.py:386
  41.9 0.8 collective-permute-done.17.refs_6_
  42.7 0.8 collective-permute-done.10.refs_2_
  43.5 1.7 %collective-permute-done.11.refs_3_ = bf16[512,128]{1,0:T(8,128)(2,1)S(1)} collective-permute-done((bf16[512,128]{1,0:T(8,128)(2,1)S(1)}, bf16[512,128]{1,0:T(8,128)(2,1)S(1)}, u32[]{:S(2)}, u32[]{:S(2)}) %collective-permute-start.11) | collective-permute-done | bytes 131104 | tf_op jit(solution)/shard_map/ppermute | solution.py:386
  45.2 1.1 %activate.1 = (bf16[512,128]{1,0:T(8,128)(2,1)}, bf16[512,128]{1,0:T(8,128)(2,1)S(1)}, bf16[640,128]{1,0:T(8,128)(2,1)S(1)}) custom-call(bf16[128,128]{1,0:T(8,128)(2,1)S(1)} %copy-done.2, bf16[512,128]{1,0:T(8,128)(2,1)S(1)} %copy-done.1, f32[512,128]{1,0:T(8,128)S(1)} %get-tuple-element.65.refs_0_, bf16[512,128]{1,0:T(8,128)(2,1)S(1)} %collective-permute-done.9.refs_1_, ...), custom_call_target="tpu_custom_call" | custom-call | tf_op jit(solution)/shard_map/activate/pallas_call | solution.py:293
  46.3 3.5 %collective-permute-start.20 = (bf16[640,128]{1,0:T(8,128)(2,1)S(1)}, bf16[640,128]{1,0:T(8,128)(2,1)S(1)}, u32[]{:S(2)}, u32[]{:S(2)}) collective-permute-start(bf16[640,128]{1,0:T(8,128)(2,1)S(1)} %get-tuple-element.86.own.refs_0_), channel_id=1, source_target_pairs={{0,3},{1,0},{2,1},{3,2},{4,7},{5,4},{6,5},{7,6},{8,11},{9,8},{10,9... | collective-permute-start | bytes 491528 | tf_op jit(solution)/shard_map/ppermute | solution.py:386
  49.8 0.6 collective-permute-start.18
  50.4 0.8 collective-permute-start.23
  51.2 0.8 collective-permute-start.22
  51.9 4.3 %collective-permute-done.20.refs_2_ = bf16[640,128]{1,0:T(8,128)(2,1)S(1)} collective-permute-done((bf16[640,128]{1,0:T(8,128)(2,1)S(1)}, bf16[640,128]{1,0:T(8,128)(2,1)S(1)}, u32[]{:S(2)}, u32[]{:S(2)}) %collective-permute-start.20) | collective-permute-done | bytes 163872 | tf_op jit(solution)/shard_map/ppermute | solution.py:386
  56.3 3.2 %collective-permute-done.18.refs_0_ = bf16[640,128]{1,0:T(8,128)(2,1)S(1)} collective-permute-done((bf16[640,128]{1,0:T(8,128)(2,1)S(1)}, bf16[640,128]{1,0:T(8,128)(2,1)S(1)}, u32[]{:S(2)}, u32[]{:S(2)}) %collective-permute-start.18) | collective-permute-done | bytes 163872 | tf_op jit(solution)/shard_map/ppermute | solution.py:386
  59.5 0.1 collective-permute-start.28
  59.6 1.5 %collective-permute-start.27 = (bf16[1664,128]{1,0:T(8,128)(2,1)S(1)}, bf16[1664,128]{1,0:T(8,128)(2,1)S(1)}, u32[]{:S(2)}, u32[]{:S(2)}) collective-permute-start(bf16[1664,128]{1,0:T(8,128)(2,1)S(1)} %merge_z.1.refs_1_.rest), channel_id=1, source_target_pairs={{0,4},{1,5},{2,6},{3,7},{4,8},{5,9},{6,10},{7,11},{8,12},{9,13},{1... | collective-permute-start | bytes 1277960 | tf_op jit(solution)/shard_map/ppermute | solution.py:382
  61.1 1.6 %collective-permute-start.26 = (bf16[640,128]{1,0:T(8,128)(2,1)S(1)}, bf16[640,128]{1,0:T(8,128)(2,1)S(1)}, u32[]{:S(2)}, u32[]{:S(2)}) collective-permute-start(bf16[640,128]{1,0:T(8,128)(2,1)S(1)} %collective-permute-done.23.refs_4_.level), channel_id=1, source_target_pairs={{0,3},{1,0},{2,1},{3,2},{4,7},{5,4},{6,5},{7,6},{8,11},{9,8},{10,9... | collective-permute-start | bytes 491528 | tf_op jit(solution)/shard_map/ppermute | solution.py:386
  62.6 0.7 collective-permute-start.24
  63.3 3.4 %backward_early.1.before = f32[33,128,128]{2,1,0:T(8,128)S(1)} custom-call(s32[1,640]{1,0:T(1,128)S(1)} %get-tuple-element.85.codes_ref, bf16[512,128,128]{2,1,0:T(8,128)(2,1)S(1)} %get-tuple-element.59.adj_ref, bf16[640,128]{1,0:T(8,128)(2,1)S(1)} %get-tuple-element.86.own.refs_0_, bf16[1664,128]{1,0:T(8,128)(2,1)S(1)} %merge_z.1.refs_1_.rest, ...), custom_call_target="tpu_custom_call" | custom-call | flops 3221225472 | bytes 7864320 | tf_op jit(solution)/shard_map/backward_early/pallas_call | solution.py:147
  66.7 1.7 %collective-permute-done.25.refs_1_ = bf16[640,128]{1,0:T(8,128)(2,1)S(1)} collective-permute-done((bf16[640,128]{1,0:T(8,128)(2,1)S(1)}, bf16[640,128]{1,0:T(8,128)(2,1)S(1)}, u32[]{:S(2)}, u32[]{:S(2)}) %collective-permute-start.25) | collective-permute-done | bytes 163872 | tf_op jit(solution)/shard_map/ppermute | solution.py:386
  68.4 2.8 %collective-permute-done.24.refs_0_ = bf16[640,128]{1,0:T(8,128)(2,1)S(1)} collective-permute-done((bf16[640,128]{1,0:T(8,128)(2,1)S(1)}, bf16[640,128]{1,0:T(8,128)(2,1)S(1)}, u32[]{:S(2)}, u32[]{:S(2)}) %collective-permute-start.24) | collective-permute-done | bytes 163872 | tf_op jit(solution)/shard_map/ppermute | solution.py:386
  71.2 2.6 %backward_other.1 = (f32[2176,128]{1,0:T(8,128)S(1)}, f32[128,128]{1,0:T(8,128)S(1)}, bf16[36,128,128]{2,1,0:T(8,128)(2,1)S(1)}) custom-call(s32[1,640]{1,0:T(1,128)S(1)} %get-tuple-element.88.codes_ref, bf16[512,128,128]{2,1,0:T(8,128)(2,1)S(1)} %get-tuple-element.59.adj_ref, f32[33,128,128]{2,1,0:T(8,128)S(1)} %backward_early.1.before, ...), custom_call_target="tpu_custom_call" | custom-call | flops 2576980480 | bytes 6291456 | tf_op jit(solution)/shard_map/backward_other/pallas_call | solution.py:147
  73.7 3.0 %collective-permute-start.29 = (f32[2176,128]{1,0:T(8,128)S(1)}, f32[2176,128]{1,0:T(8,128)S(1)}, u32[]{:S(2)}, u32[]{:S(2)}) collective-permute-start(f32[2176,128]{1,0:T(8,128)S(1)} %get-tuple-element.91), channel_id=1, source_target_pairs={{0,16},{16,0},{32,48},{48,32},{64,80},{80,64},{96,112},{112,96},{1... | collective-permute-start | bytes 3342344 | tf_op jit(solution)/shard_map/ppermute | solution.py:394
  76.7 2.5 %backward_own.1.keep = f32[2048,128]{1,0:T(8,128)S(1)} custom-call(s32[1,640]{1,0:T(1,128)S(1)} %get-tuple-element.84.codes_ref, bf16[512,128,128]{2,1,0:T(8,128)(2,1)S(1)} %get-tuple-element.59.adj_ref, f32[33,128,128]{2,1,0:T(8,128)S(1)} %backward_early.1.before, bf16[36,128,128]{2,1,0:T(8,128)(2,1)S(1)} %get-tuple-element.89.slopes), custom_call_target="tpu_custom_call" | custom-call | flops 2576980480 | bytes 6291456 | tf_op jit(solution)/shard_map/backward_own/pallas_call | solution.py:147
  79.2 0.1 add_core.1
  79.3 2.1 %collective-permute-start.30 = (bf16[640,128]{1,0:T(8,128)(2,1)S(1)}, bf16[640,128]{1,0:T(8,128)(2,1)S(1)}, u32[]{:S(2)}, u32[]{:S(2)}) collective-permute-start(bf16[640,128]{1,0:T(8,128)(2,1)S(1)} %get-tuple-element.94), channel_id=1, source_target_pairs={{0,64},{16,80},{32,96},{48,112},{64,0},{80,16},{96,32},{112,48},{1... | collective-permute-start | bytes 491528 | tf_op jit(solution)/shard_map/ppermute | solution.py:390
  81.4 0.9 collective-permute-start.31
  82.3 2.3 %collective-permute-start.32 = (bf16[640,128]{1,0:T(8,128)(2,1)S(1)}, bf16[640,128]{1,0:T(8,128)(2,1)S(1)}, u32[]{:S(2)}, u32[]{:S(2)}) collective-permute-start(bf16[640,128]{1,0:T(8,128)(2,1)S(1)} %get-tuple-element.96), channel_id=1, source_target_pairs={{0,96},{16,112},{32,0},{48,16},{64,32},{80,48},{96,64},{112,80},{1... | collective-permute-start | bytes 491528 | tf_op jit(solution)/shard_map/ppermute | solution.py:390
  84.6 1.8 %collective-permute-done.30.refs_0_ = bf16[640,128]{1,0:T(8,128)(2,1)S(1)} collective-permute-done((bf16[640,128]{1,0:T(8,128)(2,1)S(1)}, bf16[640,128]{1,0:T(8,128)(2,1)S(1)}, u32[]{:S(2)}, u32[]{:S(2)}) %collective-permute-start.30) | collective-permute-done | bytes 163872 | tf_op jit(solution)/shard_map/ppermute | solution.py:390
  86.4 4.1 %collective-permute-done.31.refs_1_ = bf16[640,128]{1,0:T(8,128)(2,1)S(1)} collective-permute-done((bf16[640,128]{1,0:T(8,128)(2,1)S(1)}, bf16[640,128]{1,0:T(8,128)(2,1)S(1)}, u32[]{:S(2)}, u32[]{:S(2)}) %collective-permute-start.31) | collective-permute-done | bytes 163872 | tf_op jit(solution)/shard_map/ppermute | solution.py:390
  90.5 1.0 %finish.1 = (bf16[512,128]{1,0:T(8,128)(2,1)}, f32[128,128]{1,0:T(8,128)}) custom-call(bf16[128,128]{1,0:T(8,128)(2,1)S(1)} %copy-done.2, f32[512,128]{1,0:T(8,128)S(1)} %get-tuple-element.92.own, f32[128,128]{1,0:T(8,128)S(1)} %get-tuple-element.93.wown, bf16[640,128]{1,0:T(8,128)(2,1)S(1)} %collective-permute-done.30.refs_0_, ...), custom_call_target="tpu_custom_call" | custom-call | tf_op jit(solution)/shard_map/finish/pallas_call | solution.py:368
  (22 shorter events, 0.1 us)
Async XLA Ops:
  0.6 13.4 %collective-permute-start.2 = (bf16[512,128]{1,0:T(8,128)(2,1)}, bf16[512,128]{1,0:T(8,128)(2,1)S(1)}, u32[]{:S(2)}, u32[]{:S(2)}) collective-permute-start(bf16[512,128]{1,0:T(8,128)(2,1)} %refs_0_.1), channel_id=1, source_target_pairs={{0,96},{16,112},{32,0},{48,16},{64,32},{80,48},{96,64},{112,80},{1... | collective-permute-start | bytes 393224 | tf_op jit(solution)/shard_map/ppermute | solution.py:390
  4.3 9.8 %collective-permute-start.1 = (bf16[512,128]{1,0:T(8,128)(2,1)}, bf16[512,128]{1,0:T(8,128)(2,1)S(1)}, u32[]{:S(2)}, u32[]{:S(2)}) collective-permute-start(bf16[512,128]{1,0:T(8,128)(2,1)} %refs_0_.1), channel_id=1, source_target_pairs={{0,64},{16,80},{32,96},{48,112},{64,0},{80,16},{96,32},{112,48},{1... | collective-permute-start | bytes 393224 | tf_op jit(solution)/shard_map/ppermute | solution.py:390
  4.6 9.5 %collective-permute-start = (bf16[512,128]{1,0:T(8,128)(2,1)}, bf16[512,128]{1,0:T(8,128)(2,1)S(1)}, u32[]{:S(2)}, u32[]{:S(2)}) collective-permute-start(bf16[512,128]{1,0:T(8,128)(2,1)} %refs_0_.1), channel_id=1, source_target_pairs={{0,32},{16,48},{32,64},{48,80},{64,96},{80,112},{96,0},{112,16},{1... | collective-permute-start | bytes 393224 | tf_op jit(solution)/shard_map/ppermute | solution.py:390
  5.3 9.9 %collective-permute-start.3 = (bf16[512,128]{1,0:T(8,128)(2,1)}, bf16[512,128]{1,0:T(8,128)(2,1)S(1)}, u32[]{:S(2)}, u32[]{:S(2)}) collective-permute-start(bf16[512,128]{1,0:T(8,128)(2,1)} %refs_0_.1), channel_id=1, source_target_pairs={{0,16},{16,0},{32,48},{48,32},{64,80},{80,64},{96,112},{112,96},{1... | collective-permute-start | bytes 393224 | tf_op jit(solution)/shard_map/ppermute | solution.py:394
  8.2 8.1 %copy-start = (bf16[512,128]{1,0:T(8,128)(2,1)S(1)}, bf16[512,128]{1,0:T(8,128)(2,1)}, u32[]{:S(2)}) copy-start(bf16[512,128]{1,0:T(8,128)(2,1)} %refs_0_.1) | copy-start | bytes 393220
  14.1 1.6 %collective-permute-start.4 = (bf16[512,128]{1,0:T(8,128)(2,1)S(1)}, bf16[512,128]{1,0:T(8,128)(2,1)S(1)}, u32[]{:S(2)}, u32[]{:S(2)}) collective-permute-start(bf16[512,128]{1,0:T(8,128)(2,1)S(1)} %collective-permute-done.refs_1_), channel_id=1, source_target_pairs={{0,16},{16,0},{32,48},{48,32},{64,80},{80,64},{96,112},{112,96},{1... | collective-permute-start | bytes 393224 | tf_op jit(solution)/shard_map/ppermute | solution.py:394
  14.7 1.3 %collective-permute-start.5 = (bf16[512,128]{1,0:T(8,128)(2,1)S(1)}, bf16[512,128]{1,0:T(8,128)(2,1)S(1)}, u32[]{:S(2)}, u32[]{:S(2)}) collective-permute-start(bf16[512,128]{1,0:T(8,128)(2,1)S(1)} %collective-permute-done.1.refs_2_), channel_id=1, source_target_pairs={{0,16},{16,0},{32,48},{48,32},{64,80},{80,64},{96,112},{112,96},{1... | collective-permute-start | bytes 393224 | tf_op jit(solution)/shard_map/ppermute | solution.py:394
  14.7 1.5 %collective-permute-start.6 = (bf16[512,128]{1,0:T(8,128)(2,1)S(1)}, bf16[512,128]{1,0:T(8,128)(2,1)S(1)}, u32[]{:S(2)}, u32[]{:S(2)}) collective-permute-start(bf16[512,128]{1,0:T(8,128)(2,1)S(1)} %collective-permute-done.2.refs_3_), channel_id=1, source_target_pairs={{0,16},{16,0},{32,48},{48,32},{64,80},{80,64},{96,112},{112,96},{1... | collective-permute-start | bytes 393224 | tf_op jit(solution)/shard_map/ppermute | solution.py:394
  19.7 13.5 %collective-permute-start.7 = (bf16[1536,128]{1,0:T(8,128)(2,1)S(1)}, bf16[1536,128]{1,0:T(8,128)(2,1)S(1)}, u32[]{:S(2)}, u32[]{:S(2)}) collective-permute-start(bf16[1536,128]{1,0:T(8,128)(2,1)S(1)} %get-tuple-element.69), channel_id=1, source_target_pairs={{0,4},{1,5},{2,6},{3,7},{4,8},{5,9},{6,10},{7,11},{8,12},{9,13},{1... | collective-permute-start | bytes 1179656 | tf_op jit(solution)/shard_map/ppermute | solution.py:382
  20.1 13.1 %collective-permute-start.8 = (bf16[1536,128]{1,0:T(8,128)(2,1)S(1)}, bf16[1536,128]{1,0:T(8,128)(2,1)S(1)}, u32[]{:S(2)}, u32[]{:S(2)}) collective-permute-start(bf16[1536,128]{1,0:T(8,128)(2,1)S(1)} %get-tuple-element.70), channel_id=1, source_target_pairs={{0,12},{1,13},{2,14},{3,15},{4,0},{5,1},{6,2},{7,3},{8,4},{9,5},{1... | collective-permute-start | bytes 1179656 | tf_op jit(solution)/shard_map/ppermute | solution.py:382
  25.1 9.0 %collective-permute-start.14 = (bf16[512,128]{1,0:T(8,128)(2,1)S(1)}, bf16[512,128]{1,0:T(8,128)(2,1)S(1)}, u32[]{:S(2)}, u32[]{:S(2)}) collective-permute-start(bf16[512,128]{1,0:T(8,128)(2,1)S(1)} %get-tuple-element.80), channel_id=1, source_target_pairs={{0,1},{1,2},{2,3},{3,0},{4,5},{5,6},{6,7},{7,4},{8,9},{9,10},{10,1... | collective-permute-start | bytes 393224 | tf_op jit(solution)/shard_map/ppermute | solution.py:386
  26.2 10.0 %collective-permute-start.15 = (bf16[512,128]{1,0:T(8,128)(2,1)S(1)}, bf16[512,128]{1,0:T(8,128)(2,1)S(1)}, u32[]{:S(2)}, u32[]{:S(2)}) collective-permute-start(bf16[512,128]{1,0:T(8,128)(2,1)S(1)} %get-tuple-element.81), channel_id=1, source_target_pairs={{0,2},{1,3},{2,0},{3,1},{4,6},{5,7},{6,4},{7,5},{8,10},{9,11},{10,... | collective-permute-start | bytes 393224 | tf_op jit(solution)/shard_map/ppermute | solution.py:386
  29.0 7.1 %collective-permute-start.16 = (bf16[512,128]{1,0:T(8,128)(2,1)S(1)}, bf16[512,128]{1,0:T(8,128)(2,1)S(1)}, u32[]{:S(2)}, u32[]{:S(2)}) collective-permute-start(bf16[512,128]{1,0:T(8,128)(2,1)S(1)} %get-tuple-element.82), channel_id=1, source_target_pairs={{0,3},{1,0},{2,1},{3,2},{4,7},{5,4},{6,5},{7,6},{8,11},{9,8},{10,9... | collective-permute-start | bytes 393224 | tf_op jit(solution)/shard_map/ppermute | solution.py:386
  33.1 12.1 %copy-start.1 = (bf16[512,128]{1,0:T(8,128)(2,1)S(1)}, bf16[512,128]{1,0:T(8,128)(2,1)}, u32[]{:S(2)}) copy-start(bf16[512,128]{1,0:T(8,128)(2,1)} %grad_ref.1) | copy-start | bytes 393220
  33.2 12.1 %copy-start.2 = (bf16[128,128]{1,0:T(8,128)(2,1)S(1)}, bf16[128,128]{1,0:T(8,128)(2,1)}, u32[]{:S(2)}) copy-start(bf16[128,128]{1,0:T(8,128)(2,1)} %weight_ref.3) | copy-start | bytes 98308
  33.3 7.1 %collective-permute-start.9 = (bf16[512,128]{1,0:T(8,128)(2,1)S(1)}, bf16[512,128]{1,0:T(8,128)(2,1)S(1)}, u32[]{:S(2)}, u32[]{:S(2)}) collective-permute-start(bf16[512,128]{1,0:T(8,128)(2,1)S(1)} %get-tuple-element.74), channel_id=1, source_target_pairs={{0,1},{1,2},{2,3},{3,0},{4,5},{5,6},{6,7},{7,4},{8,9},{9,10},{10,1... | collective-permute-start | bytes 393224 | tf_op jit(solution)/shard_map/ppermute | solution.py:386
  33.4 8.5 %collective-permute-start.12 = (bf16[512,128]{1,0:T(8,128)(2,1)S(1)}, bf16[512,128]{1,0:T(8,128)(2,1)S(1)}, u32[]{:S(2)}, u32[]{:S(2)}) collective-permute-start(bf16[512,128]{1,0:T(8,128)(2,1)S(1)} %get-tuple-element.77), channel_id=1, source_target_pairs={{0,4},{1,5},{2,6},{3,7},{4,8},{5,9},{6,10},{7,11},{8,12},{9,13},{1... | collective-permute-start | bytes 393224 | tf_op jit(solution)/shard_map/ppermute | solution.py:382
  34.1 7.8 %collective-permute-start.13 = (bf16[512,128]{1,0:T(8,128)(2,1)S(1)}, bf16[512,128]{1,0:T(8,128)(2,1)S(1)}, u32[]{:S(2)}, u32[]{:S(2)}) collective-permute-start(bf16[512,128]{1,0:T(8,128)(2,1)S(1)} %get-tuple-element.78), channel_id=1, source_target_pairs={{0,12},{1,13},{2,14},{3,15},{4,0},{5,1},{6,2},{7,3},{8,4},{9,5},{1... | collective-permute-start | bytes 393224 | tf_op jit(solution)/shard_map/ppermute | solution.py:382
  36.2 6.4 %collective-permute-start.17 = (bf16[512,128]{1,0:T(8,128)(2,1)S(1)}, bf16[512,128]{1,0:T(8,128)(2,1)S(1)}, u32[]{:S(2)}, u32[]{:S(2)}) collective-permute-start(bf16[512,128]{1,0:T(8,128)(2,1)S(1)} %add_z.1), channel_id=1, source_target_pairs={{0,8},{1,9},{2,10},{3,11},{4,12},{5,13},{6,14},{7,15},{8,0},{9,1},... | collective-permute-start | bytes 393224 | tf_op jit(solution)/shard_map/ppermute | solution.py:382
  37.9 5.6 %collective-permute-start.10 = (bf16[512,128]{1,0:T(8,128)(2,1)S(1)}, bf16[512,128]{1,0:T(8,128)(2,1)S(1)}, u32[]{:S(2)}, u32[]{:S(2)}) collective-permute-start(bf16[512,128]{1,0:T(8,128)(2,1)S(1)} %get-tuple-element.75), channel_id=1, source_target_pairs={{0,2},{1,3},{2,0},{3,1},{4,6},{5,7},{6,4},{7,5},{8,10},{9,11},{10,... | collective-permute-start | bytes 393224 | tf_op jit(solution)/shard_map/ppermute | solution.py:386
  40.4 4.8 %collective-permute-start.11 = (bf16[512,128]{1,0:T(8,128)(2,1)S(1)}, bf16[512,128]{1,0:T(8,128)(2,1)S(1)}, u32[]{:S(2)}, u32[]{:S(2)}) collective-permute-start(bf16[512,128]{1,0:T(8,128)(2,1)S(1)} %get-tuple-element.76), channel_id=1, source_target_pairs={{0,3},{1,0},{2,1},{3,2},{4,7},{5,4},{6,5},{7,6},{8,11},{9,8},{10,9... | collective-permute-start | bytes 393224 | tf_op jit(solution)/shard_map/ppermute | solution.py:386
  46.3 10.0 %collective-permute-start.20 = (bf16[640,128]{1,0:T(8,128)(2,1)S(1)}, bf16[640,128]{1,0:T(8,128)(2,1)S(1)}, u32[]{:S(2)}, u32[]{:S(2)}) collective-permute-start(bf16[640,128]{1,0:T(8,128)(2,1)S(1)} %get-tuple-element.86.own.refs_0_), channel_id=1, source_target_pairs={{0,3},{1,0},{2,1},{3,2},{4,7},{5,4},{6,5},{7,6},{8,11},{9,8},{10,9... | collective-permute-start | bytes 491528 | tf_op jit(solution)/shard_map/ppermute | solution.py:386
  49.8 6.5 %collective-permute-start.19 = (bf16[640,128]{1,0:T(8,128)(2,1)S(1)}, bf16[640,128]{1,0:T(8,128)(2,1)S(1)}, u32[]{:S(2)}, u32[]{:S(2)}) collective-permute-start(bf16[640,128]{1,0:T(8,128)(2,1)S(1)} %get-tuple-element.86.own.refs_0_), channel_id=1, source_target_pairs={{0,2},{1,3},{2,0},{3,1},{4,6},{5,7},{6,4},{7,5},{8,10},{9,11},{10,... | collective-permute-start | bytes 491528 | tf_op jit(solution)/shard_map/ppermute | solution.py:386
  49.8 9.7 %collective-permute-start.18 = (bf16[640,128]{1,0:T(8,128)(2,1)S(1)}, bf16[640,128]{1,0:T(8,128)(2,1)S(1)}, u32[]{:S(2)}, u32[]{:S(2)}) collective-permute-start(bf16[640,128]{1,0:T(8,128)(2,1)S(1)} %get-tuple-element.86.own.refs_0_), channel_id=1, source_target_pairs={{0,1},{1,2},{2,3},{3,0},{4,5},{5,6},{6,7},{7,4},{8,9},{9,10},{10,1... | collective-permute-start | bytes 491528 | tf_op jit(solution)/shard_map/ppermute | solution.py:386
  50.4 10.7 %collective-permute-start.23 = (bf16[640,128]{1,0:T(8,128)(2,1)S(1)}, bf16[640,128]{1,0:T(8,128)(2,1)S(1)}, u32[]{:S(2)}, u32[]{:S(2)}) collective-permute-start(bf16[640,128]{1,0:T(8,128)(2,1)S(1)} %get-tuple-element.86.own.refs_0_), channel_id=1, source_target_pairs={{0,8},{1,9},{2,10},{3,11},{4,12},{5,13},{6,14},{7,15},{8,0},{9,1},... | collective-permute-start | bytes 491528 | tf_op jit(solution)/shard_map/ppermute | solution.py:382
  51.2 11.4 %collective-permute-start.22 = (bf16[512,128]{1,0:T(8,128)(2,1)S(1)}, bf16[512,128]{1,0:T(8,128)(2,1)S(1)}, u32[]{:S(2)}, u32[]{:S(2)}) collective-permute-start(bf16[512,128]{1,0:T(8,128)(2,1)S(1)} %get-tuple-element.87), channel_id=1, source_target_pairs={{0,12},{1,13},{2,14},{3,15},{4,0},{5,1},{6,2},{7,3},{8,4},{9,5},{1... | collective-permute-start | bytes 393224 | tf_op jit(solution)/shard_map/ppermute | solution.py:382
  56.3 6.4 %collective-permute-start.21 = (bf16[512,128]{1,0:T(8,128)(2,1)S(1)}, bf16[512,128]{1,0:T(8,128)(2,1)S(1)}, u32[]{:S(2)}, u32[]{:S(2)}) collective-permute-start(bf16[512,128]{1,0:T(8,128)(2,1)S(1)} %get-tuple-element.87), channel_id=1, source_target_pairs={{0,4},{1,5},{2,6},{3,7},{4,8},{5,9},{6,10},{7,11},{8,12},{9,13},{1... | collective-permute-start | bytes 393224 | tf_op jit(solution)/shard_map/ppermute | solution.py:382
  59.5 11.6 %collective-permute-start.28 = (bf16[1664,128]{1,0:T(8,128)(2,1)S(1)}, bf16[1664,128]{1,0:T(8,128)(2,1)S(1)}, u32[]{:S(2)}, u32[]{:S(2)}) collective-permute-start(bf16[1664,128]{1,0:T(8,128)(2,1)S(1)} %merge_z.1.refs_1_.rest), channel_id=1, source_target_pairs={{0,12},{1,13},{2,14},{3,15},{4,0},{5,1},{6,2},{7,3},{8,4},{9,5},{1... | collective-permute-start | bytes 1277960 | tf_op jit(solution)/shard_map/ppermute | solution.py:382
  59.6 11.6 %collective-permute-start.27 = (bf16[1664,128]{1,0:T(8,128)(2,1)S(1)}, bf16[1664,128]{1,0:T(8,128)(2,1)S(1)}, u32[]{:S(2)}, u32[]{:S(2)}) collective-permute-start(bf16[1664,128]{1,0:T(8,128)(2,1)S(1)} %merge_z.1.refs_1_.rest), channel_id=1, source_target_pairs={{0,4},{1,5},{2,6},{3,7},{4,8},{5,9},{6,10},{7,11},{8,12},{9,13},{1... | collective-permute-start | bytes 1277960 | tf_op jit(solution)/shard_map/ppermute | solution.py:382
  61.1 5.6 %collective-permute-start.26 = (bf16[640,128]{1,0:T(8,128)(2,1)S(1)}, bf16[640,128]{1,0:T(8,128)(2,1)S(1)}, u32[]{:S(2)}, u32[]{:S(2)}) collective-permute-start(bf16[640,128]{1,0:T(8,128)(2,1)S(1)} %collective-permute-done.23.refs_4_.level), channel_id=1, source_target_pairs={{0,3},{1,0},{2,1},{3,2},{4,7},{5,4},{6,5},{7,6},{8,11},{9,8},{10,9... | collective-permute-start | bytes 491528 | tf_op jit(solution)/shard_map/ppermute | solution.py:386
  62.6 5.8 %collective-permute-start.25 = (bf16[640,128]{1,0:T(8,128)(2,1)S(1)}, bf16[640,128]{1,0:T(8,128)(2,1)S(1)}, u32[]{:S(2)}, u32[]{:S(2)}) collective-permute-start(bf16[640,128]{1,0:T(8,128)(2,1)S(1)} %collective-permute-done.23.refs_4_.level), channel_id=1, source_target_pairs={{0,2},{1,3},{2,0},{3,1},{4,6},{5,7},{6,4},{7,5},{8,10},{9,11},{10,... | collective-permute-start | bytes 491528 | tf_op jit(solution)/shard_map/ppermute | solution.py:386
  62.6 8.5 %collective-permute-start.24 = (bf16[640,128]{1,0:T(8,128)(2,1)S(1)}, bf16[640,128]{1,0:T(8,128)(2,1)S(1)}, u32[]{:S(2)}, u32[]{:S(2)}) collective-permute-start(bf16[640,128]{1,0:T(8,128)(2,1)S(1)} %collective-permute-done.23.refs_4_.level), channel_id=1, source_target_pairs={{0,1},{1,2},{2,3},{3,0},{4,5},{5,6},{6,7},{7,4},{8,9},{9,10},{10,1... | collective-permute-start | bytes 491528 | tf_op jit(solution)/shard_map/ppermute | solution.py:386
  73.7 5.4 %collective-permute-start.29 = (f32[2176,128]{1,0:T(8,128)S(1)}, f32[2176,128]{1,0:T(8,128)S(1)}, u32[]{:S(2)}, u32[]{:S(2)}) collective-permute-start(f32[2176,128]{1,0:T(8,128)S(1)} %get-tuple-element.91), channel_id=1, source_target_pairs={{0,16},{16,0},{32,48},{48,32},{64,80},{80,64},{96,112},{112,96},{1... | collective-permute-start | bytes 3342344 | tf_op jit(solution)/shard_map/ppermute | solution.py:394
  79.3 7.1 %collective-permute-start.30 = (bf16[640,128]{1,0:T(8,128)(2,1)S(1)}, bf16[640,128]{1,0:T(8,128)(2,1)S(1)}, u32[]{:S(2)}, u32[]{:S(2)}) collective-permute-start(bf16[640,128]{1,0:T(8,128)(2,1)S(1)} %get-tuple-element.94), channel_id=1, source_target_pairs={{0,64},{16,80},{32,96},{48,112},{64,0},{80,16},{96,32},{112,48},{1... | collective-permute-start | bytes 491528 | tf_op jit(solution)/shard_map/ppermute | solution.py:390
  81.4 9.2 %collective-permute-start.31 = (bf16[640,128]{1,0:T(8,128)(2,1)S(1)}, bf16[640,128]{1,0:T(8,128)(2,1)S(1)}, u32[]{:S(2)}, u32[]{:S(2)}) collective-permute-start(bf16[640,128]{1,0:T(8,128)(2,1)S(1)} %get-tuple-element.95), channel_id=1, source_target_pairs={{0,32},{16,48},{32,64},{48,80},{64,96},{80,112},{96,0},{112,16},{1... | collective-permute-start | bytes 491528 | tf_op jit(solution)/shard_map/ppermute | solution.py:390
  82.3 8.2 %collective-permute-start.32 = (bf16[640,128]{1,0:T(8,128)(2,1)S(1)}, bf16[640,128]{1,0:T(8,128)(2,1)S(1)}, u32[]{:S(2)}, u32[]{:S(2)}) collective-permute-start(bf16[640,128]{1,0:T(8,128)(2,1)S(1)} %get-tuple-element.96), channel_id=1, source_target_pairs={{0,96},{16,112},{32,0},{48,16},{64,32},{80,48},{96,64},{112,80},{1... | collective-permute-start | bytes 491528 | tf_op jit(solution)/shard_map/ppermute | solution.py:390

commit v2 on v0

--- a/solution.py
+++ b/solution.py
@@ -31,12 +31,19 @@
 LISTS = 6
 FAR = (NZ - 1) * OWN
 OTHER = NY * OWN
+LOADS = 8
 
 
 def prepare_kernel(packed_ref, adj_ref, blocks_ref, *refs):
-    codes_refs, sem = refs[:-1], refs[-1]
-    copy = pltpu.make_async_copy(adj_ref, blocks_ref, sem)
-    copy.start()
+    codes_refs, sems = refs[:-1], refs[-1]
+    share = adj_ref.shape[0] // LOADS
+    copies = [
+        pltpu.make_async_copy(adj_ref.at[pl.ds(i * share, share)], blocks_ref.at[pl.ds(i * share, share)], sems.at[i])
+        for i in range(LOADS)
+    ]
+    live = jnp.sum((packed_ref[...] >= 0).astype(F32)).astype(jnp.int32)
+    for i, copy in enumerate(copies):
+        pl.when(live > i * share)(copy.start)
     row, col = lax.axis_index("row"), lax.axis_index("col")
     y, core = row >> 1, row & 1
     x, z = col >> 2, col & 3
@@ -108,7 +115,8 @@
     ):
         codes_refs[q][:, 0:capacity] = jnp.where(where < count, lists[q], 512.0 * idle).astype(jnp.int32)
         codes_refs[q][:, capacity : capacity + BLK] = jnp.broadcast_to(count, (1, BLK)).astype(jnp.int32)
-    copy.wait()
+    for i, copy in enumerate(copies):
+        pl.when(live > i * share)(copy.wait)
 
 
 def prepare(adjacency, packed):
@@ -121,7 +129,7 @@
         + [jax.ShapeDtypeStruct((1, capacity + BLK), jnp.int32)] * LISTS,
         in_specs=vmem_specs(1) + [pl.BlockSpec(memory_space=pl.ANY)],
         out_specs=vmem_specs(1 + LISTS),
-        scratch_shapes=[pltpu.SemaphoreType.DMA],
+        scratch_shapes=[pltpu.SemaphoreType.DMA((LOADS,))],
         compiler_params=params(),
         cost_estimate=pl.CostEstimate(flops=0, bytes_accessed=2 * adjacency.size * 2, transcendentals=0),
         name="prepare",

time: 92.7 us -> 93.4 us (level); the launches traced: 92.6 us -> 95 us
  Pallas kernels: 28.7 us -> 23.7 us
  waiting for transfers between devices: 17.1 us -> 21.9 us
  starting transfers between devices: 44.7 us -> 47.2 us
    ppermute x10, starting transfers between devices: 18 us -> 9.57 us  [shift_x(): lax.ppermute(a, 'col', [(i, (i // NZ + d) % NX * NZ + i % NZ) for i in ra...]
    ppermute x6, starting transfers between devices: 7.83 us -> 14.1 us  [shift_y(): lax.ppermute(a, 'row', [(i, (i // 2 + d) % NY * 2 + i % 2) for i in range...]
    ppermute x10, waiting for transfers between devices: 1.95 us -> 5.99 us  [shift_x(): lax.ppermute(a, 'col', [(i, (i // NZ + d) % NX * NZ + i % NZ) for i in ra...]
    pallas_call x6, Pallas kernels: 20.5 us -> 16.6 us  [sparse_call(): pl.pallas_call(kernel, out_shape=[jax.ShapeDtypeStruct(shape, dtype) for...]
    ppermute x5, starting transfers between devices: 4.44 us -> 8.12 us  [swap_core(): return lax.ppermute(a, 'row', [(i, i ^ 1) for i in range(NY * 2)])]
    ppermute x12, waiting for transfers between devices: 6.11 us -> 7.81 us  [shift_z(): lax.ppermute(a, 'col', [(i, i // NZ * NZ + (i % NZ + d) % NZ) for i in ra...]
    ppermute x12, starting transfers between devices: 14.4 us -> 15.4 us  [shift_z(): lax.ppermute(a, 'col', [(i, i // NZ * NZ + (i % NZ + d) % NZ) for i in ra...]
    pallas_call x1, Pallas kernels: 5.82 us -> 4.85 us  [prepare(): pl.pallas_call(prepare_kernel, out_shape=[jax.ShapeDtypeStruct(adjacency....]
  transfers between devices with their start and end apart: 33 -> 33, of which waited for: 11 -> 15; matrix products, arithmetic and copies ran while one was open for 1% -> 1% of each run, Pallas kernels for 21% -> 16%
where the time goes in v2:
time: 93.4 us; the launch traced here: 95 us
  starting transfers between devices  47.2 us (51%)
  Pallas kernels  23.7 us (25%)
  waiting for transfers between devices  21.9 us (23%)
  between operations  1.45 us (2%)
    pallas_call x6, Pallas kernels, sparse_call(): pl.pallas_call(kernel, out_shape=[jax.ShapeDtypeStruct(shape, dtype) for...  16.6 us
    ppermute x12, starting transfers between devices, shift_z(): lax.ppermute(a, 'col', [(i, i // NZ * NZ + (i % NZ + d) % NZ) for i in ra...  15.4 us
    ppermute x6, starting transfers between devices, shift_y(): lax.ppermute(a, 'row', [(i, (i // 2 + d) % NY * 2 + i % 2) for i in range...  14.1 us
    ppermute x10, starting transfers between devices, shift_x(): lax.ppermute(a, 'col', [(i, (i // NZ + d) % NX * NZ + i % NZ) for i in ra...  9.57 us
    ppermute x5, starting transfers between devices, swap_core(): return lax.ppermute(a, 'row', [(i, i ^ 1) for i in range(NY * 2)])  8.12 us
    ppermute x12, waiting for transfers between devices, shift_z(): lax.ppermute(a, 'col', [(i, i // NZ * NZ + (i % NZ + d) % NZ) for i in ra...  7.81 us
    ppermute x6, waiting for transfers between devices, shift_y(): lax.ppermute(a, 'row', [(i, (i // 2 + d) % NY * 2 + i % 2) for i in range...  7.1 us
    ppermute x10, waiting for transfers between devices, shift_x(): lax.ppermute(a, 'col', [(i, (i // NZ + d) % NX * NZ + i % NZ) for i in ra...  5.99 us
  transfers between devices with their start and end apart: 33, of which 15 were waited for; matrix products, arithmetic and copies ran while one was open for 1% of the time, Pallas kernels for 16%

profile of v2, /device:TPU:1, one launch (start us, length us, event | category | flops | bytes accessed | tf_op | source)
XLA Modules:
  0.0 95.0 jit_solution(17910708933361199141)
XLA Ops:
  0.6 3.6 %collective-permute-start.2 = (bf16[512,128]{1,0:T(8,128)(2,1)}, bf16[512,128]{1,0:T(8,128)(2,1)S(1)}, u32[]{:S(2)}, u32[]{:S(2)}) collective-permute-start(bf16[512,128]{1,0:T(8,128)(2,1)} %refs_0_.1), channel_id=1, source_target_pairs={{0,96},{16,112},{32,0},{48,16},{64,32},{80,48},{96,64},{112,80},{1... | collective-permute-start | bytes 393224 | tf_op jit(solution)/shard_map/ppermute | solution.py:396
  4.3 0.3 collective-permute-start.1
  4.6 0.7 collective-permute-start
  5.3 1.5 %collective-permute-start.3 = (bf16[512,128]{1,0:T(8,128)(2,1)}, bf16[512,128]{1,0:T(8,128)(2,1)S(1)}, u32[]{:S(2)}, u32[]{:S(2)}) collective-permute-start(bf16[512,128]{1,0:T(8,128)(2,1)} %refs_0_.1), channel_id=1, source_target_pairs={{0,16},{16,0},{32,48},{48,32},{64,80},{80,64},{96,112},{112,96},{1... | collective-permute-start | bytes 393224 | tf_op jit(solution)/shard_map/ppermute | solution.py:400
  7.5 0.7 compare_select_fusion.packed_ref
  8.2 4.9 %prepare.1 = (bf16[512,128,128]{2,1,0:T(8,128)(2,1)S(1)}, s32[1,640]{1,0:T(1,128)S(1)}, s32[1,640]{1,0:T(1,128)S(1)}, s32[1,640]{1,0:T(1,128)S(1)}, s32[1,640]{1...) custom-call(s32[1,512]{1,0:T(1,128)S(1)} %compare_select_fusion.packed_ref, bf16[512,128,128]{2,1,0:T(8,128)(2,1)} %bitcast.5), custom_call_target="tpu_custom_call" | custom-call | bytes 33554432 | tf_op jit(solution)/shard_map/prepare/pallas_call | solution.py:124
  13.0 0.0 collective-permute-done.2.refs_3_
  13.1 0.0 collective-permute-done.1.refs_2_
  13.1 1.0 %collective-permute-done.refs_1_ = bf16[512,128]{1,0:T(8,128)(2,1)S(1)} collective-permute-done((bf16[512,128]{1,0:T(8,128)(2,1)}, bf16[512,128]{1,0:T(8,128)(2,1)S(1)}, u32[]{:S(2)}, u32[]{:S(2)}) %collective-permute-start) | collective-permute-done | bytes 131104 | tf_op jit(solution)/shard_map/ppermute | solution.py:396
  14.1 0.6 collective-permute-start.4
  14.7 0.0 collective-permute-start.5
  14.7 0.5 collective-permute-start.6
  15.2 0.0 collective-permute-done.3.refs_4_
  15.2 0.5 collective-permute-done.4.refs_5_
  15.7 0.4 collective-permute-done.5.refs_6_
  16.0 0.2 collective-permute-done.6.refs_7_
  16.2 3.5 %forward_far.1 = (bf16[32,128,128]{2,1,0:T(8,128)(2,1)S(1)}, bf16[1536,128]{1,0:T(8,128)(2,1)S(1)}, bf16[1536,128]{1,0:T(8,128)(2,1)S(1)}) custom-call(s32[1,640]{1,0:T(1,128)S(1)} %get-tuple-element.59.codes_ref, bf16[512,128,128]{2,1,0:T(8,128)(2,1)S(1)} %get-tuple-element.58.adj_ref, bf16[512,128]{1,0:T(8,128)(2,1)S(1)} %copy-done, ...), custom_call_target="tpu_custom_call" | custom-call | flops 3221225472 | bytes 7864320 | tf_op jit(solution)/shard_map/forward_far/pallas_call | solution.py:155
  19.7 1.3 %collective-permute-start.7 = (bf16[1536,128]{1,0:T(8,128)(2,1)S(1)}, bf16[1536,128]{1,0:T(8,128)(2,1)S(1)}, u32[]{:S(2)}, u32[]{:S(2)}) collective-permute-start(bf16[1536,128]{1,0:T(8,128)(2,1)S(1)} %get-tuple-element.68), channel_id=1, source_target_pairs={{0,4},{1,5},{2,6},{3,7},{4,8},{5,9},{6,10},{7,11},{8,12},{9,13},{1... | collective-permute-start | bytes 1179656 | tf_op jit(solution)/shard_map/ppermute | solution.py:388
  21.0 1.5 %collective-permute-start.8 = (bf16[1536,128]{1,0:T(8,128)(2,1)S(1)}, bf16[1536,128]{1,0:T(8,128)(2,1)S(1)}, u32[]{:S(2)}, u32[]{:S(2)}) collective-permute-start(bf16[1536,128]{1,0:T(8,128)(2,1)S(1)} %get-tuple-element.69), channel_id=1, source_target_pairs={{0,12},{1,13},{2,14},{3,15},{4,0},{5,1},{6,2},{7,3},{8,4},{9,5},{1... | collective-permute-start | bytes 1179656 | tf_op jit(solution)/shard_map/ppermute | solution.py:388
  22.5 2.1 %forward_two.1 = (f32[512,128]{1,0:T(8,128)S(1)}, bf16[512,128]{1,0:T(8,128)(2,1)S(1)}, bf16[512,128]{1,0:T(8,128)(2,1)S(1)}, bf16[512,128]{1,0:T(8,128)(2,1)S(1)}) custom-call(s32[1,640]{1,0:T(1,128)S(1)} %get-tuple-element.65.codes_ref, bf16[512,128,128]{2,1,0:T(8,128)(2,1)S(1)} %get-tuple-element.58.adj_ref, bf16[32,128,128]{2,1,0:T(8,128)(2,1)S(1)} %get-tuple-element.63.feats), custom_call_target="tpu_custom_call" | custom-call | flops 2147483648 | bytes 5242880 | tf_op jit(solution)/shard_map/forward_two/pallas_call | solution.py:155
  24.6 0.3 collective-permute-start.14
  25.0 5.6 %collective-permute-start.15 = (bf16[512,128]{1,0:T(8,128)(2,1)S(1)}, bf16[512,128]{1,0:T(8,128)(2,1)S(1)}, u32[]{:S(2)}, u32[]{:S(2)}) collective-permute-start(bf16[512,128]{1,0:T(8,128)(2,1)S(1)} %get-tuple-element.80), channel_id=1, source_target_pairs={{0,2},{1,3},{2,0},{3,1},{4,6},{5,7},{6,4},{7,5},{8,10},{9,11},{10,... | collective-permute-start | bytes 393224 | tf_op jit(solution)/shard_map/ppermute | solution.py:392
  30.6 0.0 collective-permute-start.16
  30.6 2.5 %forward_rest.1 = (f32[512,128]{1,0:T(8,128)S(1)}, f32[1536,128]{1,0:T(8,128)S(1)}, bf16[512,128]{1,0:T(8,128)(2,1)S(1)}, bf16[512,128]{1,0:T(8,128)(2,1)S(1)}) custom-call(s32[1,640]{1,0:T(1,128)S(1)} %get-tuple-element.57.codes_ref, bf16[512,128,128]{2,1,0:T(8,128)(2,1)S(1)} %get-tuple-element.58.adj_ref, bf16[32,128,128]{2,1,0:T(8,128)(2,1)S(1)} %get-tuple-element.63.feats), custom_call_target="tpu_custom_call" | custom-call | flops 3221225472 | bytes 7864320 | tf_op jit(solution)/shard_map/forward_rest/pallas_call | solution.py:155
  33.1 0.0 copy-start.1
  33.1 0.0 copy-start.2
  33.1 0.0 collective-permute-done.8.refs_2_
  33.1 0.1 add_x.1
  33.3 1.6 %collective-permute-start.9 = (bf16[512,128]{1,0:T(8,128)(2,1)S(1)}, bf16[512,128]{1,0:T(8,128)(2,1)S(1)}, u32[]{:S(2)}, u32[]{:S(2)}) collective-permute-start(bf16[512,128]{1,0:T(8,128)(2,1)S(1)} %get-tuple-element.73), channel_id=1, source_target_pairs={{0,1},{1,2},{2,3},{3,0},{4,5},{5,6},{6,7},{7,4},{8,9},{9,10},{10,1... | collective-permute-start | bytes 393224 | tf_op jit(solution)/shard_map/ppermute | solution.py:392
  34.9 2.7 %collective-permute-start.13 = (bf16[512,128]{1,0:T(8,128)(2,1)S(1)}, bf16[512,128]{1,0:T(8,128)(2,1)S(1)}, u32[]{:S(2)}, u32[]{:S(2)}) collective-permute-start(bf16[512,128]{1,0:T(8,128)(2,1)S(1)} %get-tuple-element.77), channel_id=1, source_target_pairs={{0,12},{1,13},{2,14},{3,15},{4,0},{5,1},{6,2},{7,3},{8,4},{9,5},{1... | collective-permute-start | bytes 393224 | tf_op jit(solution)/shard_map/ppermute | solution.py:388
  37.5 0.1 add_z.1
  37.6 0.1 collective-permute-start.17
  37.7 3.0 %collective-permute-start.10 = (bf16[512,128]{1,0:T(8,128)(2,1)S(1)}, bf16[512,128]{1,0:T(8,128)(2,1)S(1)}, u32[]{:S(2)}, u32[]{:S(2)}) collective-permute-start(bf16[512,128]{1,0:T(8,128)(2,1)S(1)} %get-tuple-element.74), channel_id=1, source_target_pairs={{0,2},{1,3},{2,0},{3,1},{4,6},{5,7},{6,4},{7,5},{8,10},{9,11},{10,... | collective-permute-start | bytes 393224 | tf_op jit(solution)/shard_map/ppermute | solution.py:392
  40.7 0.4 collective-permute-start.11
  41.1 2.5 %collective-permute-done.17.refs_6_ = bf16[512,128]{1,0:T(8,128)(2,1)S(1)} collective-permute-done((bf16[512,128]{1,0:T(8,128)(2,1)S(1)}, bf16[512,128]{1,0:T(8,128)(2,1)S(1)}, u32[]{:S(2)}, u32[]{:S(2)}) %collective-permute-start.17) | collective-permute-done | bytes 131104 | tf_op jit(solution)/shard_map/ppermute | solution.py:388
  43.5 1.1 %collective-permute-done.11.refs_3_ = bf16[512,128]{1,0:T(8,128)(2,1)S(1)} collective-permute-done((bf16[512,128]{1,0:T(8,128)(2,1)S(1)}, bf16[512,128]{1,0:T(8,128)(2,1)S(1)}, u32[]{:S(2)}, u32[]{:S(2)}) %collective-permute-start.11) | collective-permute-done | bytes 131104 | tf_op jit(solution)/shard_map/ppermute | solution.py:392
  44.7 1.0 %activate.1 = (bf16[512,128]{1,0:T(8,128)(2,1)}, bf16[640,128]{1,0:T(8,128)(2,1)S(1)}) custom-call(bf16[128,128]{1,0:T(8,128)(2,1)S(1)} %copy-done.2, bf16[512,128]{1,0:T(8,128)(2,1)S(1)} %copy-done.1, f32[512,128]{1,0:T(8,128)S(1)} %get-tuple-element.64.refs_0_, bf16[512,128]{1,0:T(8,128)(2,1)S(1)} %collective-permute-done.9.refs_1_, ...), custom_call_target="tpu_custom_call" | custom-call | tf_op jit(solution)/shard_map/activate/pallas_call | solution.py:300
  45.7 2.7 %collective-permute-start.20 = (bf16[640,128]{1,0:T(8,128)(2,1)S(1)}, bf16[640,128]{1,0:T(8,128)(2,1)S(1)}, u32[]{:S(2)}, u32[]{:S(2)}) collective-permute-start(bf16[640,128]{1,0:T(8,128)(2,1)S(1)} %get-tuple-element.85.own.refs_0_), channel_id=1, source_target_pairs={{0,3},{1,0},{2,1},{3,2},{4,7},{5,4},{6,5},{7,6},{8,11},{9,8},{10,9... | collective-permute-start | bytes 491528 | tf_op jit(solution)/shard_map/ppermute | solution.py:392
  48.4 0.1 collective-permute-start.19
  48.5 0.5 collective-permute-start.18
  48.9 1.6 %collective-permute-start.23 = (bf16[640,128]{1,0:T(8,128)(2,1)S(1)}, bf16[640,128]{1,0:T(8,128)(2,1)S(1)}, u32[]{:S(2)}, u32[]{:S(2)}) collective-permute-start(bf16[640,128]{1,0:T(8,128)(2,1)S(1)} %get-tuple-element.85.own.refs_0_), channel_id=1, source_target_pairs={{0,8},{1,9},{2,10},{3,11},{4,12},{5,13},{6,14},{7,15},{8,0},{9,1},... | collective-permute-start | bytes 491528 | tf_op jit(solution)/shard_map/ppermute | solution.py:388
  50.6 0.9 collective-permute-start.22
  51.4 1.0 %collective-permute-done.20.refs_2_ = bf16[640,128]{1,0:T(8,128)(2,1)S(1)} collective-permute-done((bf16[640,128]{1,0:T(8,128)(2,1)S(1)}, bf16[640,128]{1,0:T(8,128)(2,1)S(1)}, u32[]{:S(2)}, u32[]{:S(2)}) %collective-permute-start.20) | collective-permute-done | bytes 163872 | tf_op jit(solution)/shard_map/ppermute | solution.py:392
  52.4 1.8 %collective-permute-done.19.refs_1_ = bf16[640,128]{1,0:T(8,128)(2,1)S(1)} collective-permute-done((bf16[640,128]{1,0:T(8,128)(2,1)S(1)}, bf16[640,128]{1,0:T(8,128)(2,1)S(1)}, u32[]{:S(2)}, u32[]{:S(2)}) %collective-permute-start.19) | collective-permute-done | bytes 163872 | tf_op jit(solution)/shard_map/ppermute | solution.py:392
  54.1 1.5 %collective-permute-done.18.refs_0_ = bf16[640,128]{1,0:T(8,128)(2,1)S(1)} collective-permute-done((bf16[640,128]{1,0:T(8,128)(2,1)S(1)}, bf16[640,128]{1,0:T(8,128)(2,1)S(1)}, u32[]{:S(2)}, u32[]{:S(2)}) %collective-permute-start.18) | collective-permute-done | bytes 163872 | tf_op jit(solution)/shard_map/ppermute | solution.py:392
  55.7 1.2 %collective-permute-start.28 = (bf16[1664,128]{1,0:T(8,128)(2,1)S(1)}, bf16[1664,128]{1,0:T(8,128)(2,1)S(1)}, u32[]{:S(2)}, u32[]{:S(2)}) collective-permute-start(bf16[1664,128]{1,0:T(8,128)(2,1)S(1)} %merge_z.1.refs_1_.rest), channel_id=1, source_target_pairs={{0,12},{1,13},{2,14},{3,15},{4,0},{5,1},{6,2},{7,3},{8,4},{9,5},{1... | collective-permute-start | bytes 1277960 | tf_op jit(solution)/shard_map/ppermute | solution.py:388
  56.9 0.3 collective-permute-start.27
  57.2 1.1 %collective-permute-start.26 = (bf16[640,128]{1,0:T(8,128)(2,1)S(1)}, bf16[640,128]{1,0:T(8,128)(2,1)S(1)}, u32[]{:S(2)}, u32[]{:S(2)}) collective-permute-start(bf16[640,128]{1,0:T(8,128)(2,1)S(1)} %collective-permute-done.23.refs_4_.level), channel_id=1, source_target_pairs={{0,3},{1,0},{2,1},{3,2},{4,7},{5,4},{6,5},{7,6},{8,11},{9,8},{10,9... | collective-permute-start | bytes 491528 | tf_op jit(solution)/shard_map/ppermute | solution.py:392
  58.3 0.2 collective-permute-start.25
  58.5 1.3 %collective-permute-done.21.refs_2_ = bf16[640,128]{1,0:T(8,128)(2,1)S(1)} collective-permute-done((bf16[640,128]{1,0:T(8,128)(2,1)S(1)}, bf16[640,128]{1,0:T(8,128)(2,1)S(1)}, u32[]{:S(2)}, u32[]{:S(2)}) %collective-permute-start.21) | collective-permute-done | bytes 163872 | tf_op jit(solution)/shard_map/ppermute | solution.py:388
  59.8 3.4 %backward_early.1.before = f32[33,128,128]{2,1,0:T(8,128)S(1)} custom-call(s32[1,640]{1,0:T(1,128)S(1)} %get-tuple-element.84.codes_ref, bf16[512,128,128]{2,1,0:T(8,128)(2,1)S(1)} %get-tuple-element.58.adj_ref, bf16[640,128]{1,0:T(8,128)(2,1)S(1)} %get-tuple-element.85.own.refs_0_, bf16[1664,128]{1,0:T(8,128)(2,1)S(1)} %merge_z.1.refs_1_.rest, ...), custom_call_target="tpu_custom_call" | custom-call | flops 3221225472 | bytes 7864320 | tf_op jit(solution)/shard_map/backward_early/pallas_call | solution.py:155
  63.2 0.8 collective-permute-done.25.refs_1_
  64.0 1.7 %collective-permute-done.24.refs_0_ = bf16[640,128]{1,0:T(8,128)(2,1)S(1)} collective-permute-done((bf16[640,128]{1,0:T(8,128)(2,1)S(1)}, bf16[640,128]{1,0:T(8,128)(2,1)S(1)}, u32[]{:S(2)}, u32[]{:S(2)}) %collective-permute-start.24) | collective-permute-done | bytes 163872 | tf_op jit(solution)/shard_map/ppermute | solution.py:392
  65.7 2.2 %collective-permute-done.27.refs_3_ = bf16[1664,128]{1,0:T(8,128)(2,1)S(1)} collective-permute-done((bf16[1664,128]{1,0:T(8,128)(2,1)S(1)}, bf16[1664,128]{1,0:T(8,128)(2,1)S(1)}, u32[]{:S(2)}, u32[]{:S(2)}) %collective-permute-start.27) | collective-permute-done | bytes 426016 | tf_op jit(solution)/shard_map/ppermute | solution.py:388
  67.9 2.6 %backward_other.1 = (f32[2176,128]{1,0:T(8,128)S(1)}, f32[128,128]{1,0:T(8,128)S(1)}, bf16[36,128,128]{2,1,0:T(8,128)(2,1)S(1)}) custom-call(s32[1,640]{1,0:T(1,128)S(1)} %get-tuple-element.86.codes_ref, bf16[512,128,128]{2,1,0:T(8,128)(2,1)S(1)} %get-tuple-element.58.adj_ref, f32[33,128,128]{2,1,0:T(8,128)S(1)} %backward_early.1.before, ...), custom_call_target="tpu_custom_call" | custom-call | flops 2576980480 | bytes 6291456 | tf_op jit(solution)/shard_map/backward_other/pallas_call | solution.py:155
  70.5 5.5 %collective-permute-start.29 = (f32[2176,128]{1,0:T(8,128)S(1)}, f32[2176,128]{1,0:T(8,128)S(1)}, u32[]{:S(2)}, u32[]{:S(2)}) collective-permute-start(f32[2176,128]{1,0:T(8,128)S(1)} %get-tuple-element.89), channel_id=1, source_target_pairs={{0,16},{16,0},{32,48},{48,32},{64,80},{80,64},{96,112},{112,96},{1... | collective-permute-start | bytes 3342344 | tf_op jit(solution)/shard_map/ppermute | solution.py:400
  76.0 2.5 %backward_own.1.keep = f32[2048,128]{1,0:T(8,128)S(1)} custom-call(s32[1,640]{1,0:T(1,128)S(1)} %get-tuple-element.83.codes_ref, bf16[512,128,128]{2,1,0:T(8,128)(2,1)S(1)} %get-tuple-element.58.adj_ref, f32[33,128,128]{2,1,0:T(8,128)S(1)} %backward_early.1.before, bf16[36,128,128]{2,1,0:T(8,128)(2,1)S(1)} %get-tuple-element.87.slopes), custom_call_target="tpu_custom_call" | custom-call | flops 2576980480 | bytes 6291456 | tf_op jit(solution)/shard_map/backward_own/pallas_call | solution.py:155
  78.5 0.1 add_core.1
  78.6 7.0 %collective-permute-start.30 = (bf16[640,128]{1,0:T(8,128)(2,1)S(1)}, bf16[640,128]{1,0:T(8,128)(2,1)S(1)}, u32[]{:S(2)}, u32[]{:S(2)}) collective-permute-start(bf16[640,128]{1,0:T(8,128)(2,1)S(1)} %get-tuple-element.92), channel_id=1, source_target_pairs={{0,32},{16,48},{32,64},{48,80},{64,96},{80,112},{96,0},{112,16},{1... | collective-permute-start | bytes 491528 | tf_op jit(solution)/shard_map/ppermute | solution.py:396
  85.5 0.4 collective-permute-start.31
  86.0 2.0 %collective-permute-start.32 = (bf16[640,128]{1,0:T(8,128)(2,1)S(1)}, bf16[640,128]{1,0:T(8,128)(2,1)S(1)}, u32[]{:S(2)}, u32[]{:S(2)}) collective-permute-start(bf16[640,128]{1,0:T(8,128)(2,1)S(1)} %get-tuple-element.94), channel_id=1, source_target_pairs={{0,96},{16,112},{32,0},{48,16},{64,32},{80,48},{96,64},{112,80},{1... | collective-permute-start | bytes 491528 | tf_op jit(solution)/shard_map/ppermute | solution.py:396
  88.0 1.1 %collective-permute-done.30.refs_0_ = bf16[640,128]{1,0:T(8,128)(2,1)S(1)} collective-permute-done((bf16[640,128]{1,0:T(8,128)(2,1)S(1)}, bf16[640,128]{1,0:T(8,128)(2,1)S(1)}, u32[]{:S(2)}, u32[]{:S(2)}) %collective-permute-start.30) | collective-permute-done | bytes 163872 | tf_op jit(solution)/shard_map/ppermute | solution.py:396
  89.2 4.9 %collective-permute-done.31.refs_1_ = bf16[640,128]{1,0:T(8,128)(2,1)S(1)} collective-permute-done((bf16[640,128]{1,0:T(8,128)(2,1)S(1)}, bf16[640,128]{1,0:T(8,128)(2,1)S(1)}, u32[]{:S(2)}, u32[]{:S(2)}) %collective-permute-start.31) | collective-permute-done | bytes 163872 | tf_op jit(solution)/shard_map/ppermute | solution.py:396
  94.1 1.0 %finish.1 = (bf16[512,128]{1,0:T(8,128)(2,1)}, f32[128,128]{1,0:T(8,128)}) custom-call(bf16[128,128]{1,0:T(8,128)(2,1)S(1)} %copy-done.2, f32[512,128]{1,0:T(8,128)S(1)} %get-tuple-element.90.own, f32[128,128]{1,0:T(8,128)S(1)} %get-tuple-element.91.wown, bf16[640,128]{1,0:T(8,128)(2,1)S(1)} %collective-permute-done.30.refs_0_, ...), custom_call_target="tpu_custom_call" | custom-call | tf_op jit(solution)/shard_map/finish/pallas_call | solution.py:374
  (22 shorter events, 0.1 us)
Async XLA Ops:
  0.6 12.4 %collective-permute-start.2 = (bf16[512,128]{1,0:T(8,128)(2,1)}, bf16[512,128]{1,0:T(8,128)(2,1)S(1)}, u32[]{:S(2)}, u32[]{:S(2)}) collective-permute-start(bf16[512,128]{1,0:T(8,128)(2,1)} %refs_0_.1), channel_id=1, source_target_pairs={{0,96},{16,112},{32,0},{48,16},{64,32},{80,48},{96,64},{112,80},{1... | collective-permute-start | bytes 393224 | tf_op jit(solution)/shard_map/ppermute | solution.py:396
  4.3 8.8 %collective-permute-start.1 = (bf16[512,128]{1,0:T(8,128)(2,1)}, bf16[512,128]{1,0:T(8,128)(2,1)S(1)}, u32[]{:S(2)}, u32[]{:S(2)}) collective-permute-start(bf16[512,128]{1,0:T(8,128)(2,1)} %refs_0_.1), channel_id=1, source_target_pairs={{0,64},{16,80},{32,96},{48,112},{64,0},{80,16},{96,32},{112,48},{1... | collective-permute-start | bytes 393224 | tf_op jit(solution)/shard_map/ppermute | solution.py:396
  4.6 9.5 %collective-permute-start = (bf16[512,128]{1,0:T(8,128)(2,1)}, bf16[512,128]{1,0:T(8,128)(2,1)S(1)}, u32[]{:S(2)}, u32[]{:S(2)}) collective-permute-start(bf16[512,128]{1,0:T(8,128)(2,1)} %refs_0_.1), channel_id=1, source_target_pairs={{0,32},{16,48},{32,64},{48,80},{64,96},{80,112},{96,0},{112,16},{1... | collective-permute-start | bytes 393224 | tf_op jit(solution)/shard_map/ppermute | solution.py:396
  5.3 9.9 %collective-permute-start.3 = (bf16[512,128]{1,0:T(8,128)(2,1)}, bf16[512,128]{1,0:T(8,128)(2,1)S(1)}, u32[]{:S(2)}, u32[]{:S(2)}) collective-permute-start(bf16[512,128]{1,0:T(8,128)(2,1)} %refs_0_.1), channel_id=1, source_target_pairs={{0,16},{16,0},{32,48},{48,32},{64,80},{80,64},{96,112},{112,96},{1... | collective-permute-start | bytes 393224 | tf_op jit(solution)/shard_map/ppermute | solution.py:400
  8.2 8.1 %copy-start = (bf16[512,128]{1,0:T(8,128)(2,1)S(1)}, bf16[512,128]{1,0:T(8,128)(2,1)}, u32[]{:S(2)}) copy-start(bf16[512,128]{1,0:T(8,128)(2,1)} %refs_0_.1) | copy-start | bytes 393220
  14.1 1.6 %collective-permute-start.4 = (bf16[512,128]{1,0:T(8,128)(2,1)S(1)}, bf16[512,128]{1,0:T(8,128)(2,1)S(1)}, u32[]{:S(2)}, u32[]{:S(2)}) collective-permute-start(bf16[512,128]{1,0:T(8,128)(2,1)S(1)} %collective-permute-done.refs_1_), channel_id=1, source_target_pairs={{0,16},{16,0},{32,48},{48,32},{64,80},{80,64},{96,112},{112,96},{1... | collective-permute-start | bytes 393224 | tf_op jit(solution)/shard_map/ppermute | solution.py:400
  14.7 1.3 %collective-permute-start.5 = (bf16[512,128]{1,0:T(8,128)(2,1)S(1)}, bf16[512,128]{1,0:T(8,128)(2,1)S(1)}, u32[]{:S(2)}, u32[]{:S(2)}) collective-permute-start(bf16[512,128]{1,0:T(8,128)(2,1)S(1)} %collective-permute-done.1.refs_2_), channel_id=1, source_target_pairs={{0,16},{16,0},{32,48},{48,32},{64,80},{80,64},{96,112},{112,96},{1... | collective-permute-start | bytes 393224 | tf_op jit(solution)/shard_map/ppermute | solution.py:400
  14.7 1.5 %collective-permute-start.6 = (bf16[512,128]{1,0:T(8,128)(2,1)S(1)}, bf16[512,128]{1,0:T(8,128)(2,1)S(1)}, u32[]{:S(2)}, u32[]{:S(2)}) collective-permute-start(bf16[512,128]{1,0:T(8,128)(2,1)S(1)} %collective-permute-done.2.refs_3_), channel_id=1, source_target_pairs={{0,16},{16,0},{32,48},{48,32},{64,80},{80,64},{96,112},{112,96},{1... | collective-permute-start | bytes 393224 | tf_op jit(solution)/shard_map/ppermute | solution.py:400
  19.7 13.4 %collective-permute-start.7 = (bf16[1536,128]{1,0:T(8,128)(2,1)S(1)}, bf16[1536,128]{1,0:T(8,128)(2,1)S(1)}, u32[]{:S(2)}, u32[]{:S(2)}) collective-permute-start(bf16[1536,128]{1,0:T(8,128)(2,1)S(1)} %get-tuple-element.68), channel_id=1, source_target_pairs={{0,4},{1,5},{2,6},{3,7},{4,8},{5,9},{6,10},{7,11},{8,12},{9,13},{1... | collective-permute-start | bytes 1179656 | tf_op jit(solution)/shard_map/ppermute | solution.py:388
  21.0 12.2 %collective-permute-start.8 = (bf16[1536,128]{1,0:T(8,128)(2,1)S(1)}, bf16[1536,128]{1,0:T(8,128)(2,1)S(1)}, u32[]{:S(2)}, u32[]{:S(2)}) collective-permute-start(bf16[1536,128]{1,0:T(8,128)(2,1)S(1)} %get-tuple-element.69), channel_id=1, source_target_pairs={{0,12},{1,13},{2,14},{3,15},{4,0},{5,1},{6,2},{7,3},{8,4},{9,5},{1... | collective-permute-start | bytes 1179656 | tf_op jit(solution)/shard_map/ppermute | solution.py:388
  24.6 10.2 %collective-permute-start.14 = (bf16[512,128]{1,0:T(8,128)(2,1)S(1)}, bf16[512,128]{1,0:T(8,128)(2,1)S(1)}, u32[]{:S(2)}, u32[]{:S(2)}) collective-permute-start(bf16[512,128]{1,0:T(8,128)(2,1)S(1)} %get-tuple-element.79), channel_id=1, source_target_pairs={{0,1},{1,2},{2,3},{3,0},{4,5},{5,6},{6,7},{7,4},{8,9},{9,10},{10,1... | collective-permute-start | bytes 393224 | tf_op jit(solution)/shard_map/ppermute | solution.py:392
  25.0 12.6 %collective-permute-start.15 = (bf16[512,128]{1,0:T(8,128)(2,1)S(1)}, bf16[512,128]{1,0:T(8,128)(2,1)S(1)}, u32[]{:S(2)}, u32[]{:S(2)}) collective-permute-start(bf16[512,128]{1,0:T(8,128)(2,1)S(1)} %get-tuple-element.80), channel_id=1, source_target_pairs={{0,2},{1,3},{2,0},{3,1},{4,6},{5,7},{6,4},{7,5},{8,10},{9,11},{10,... | collective-permute-start | bytes 393224 | tf_op jit(solution)/shard_map/ppermute | solution.py:392
  30.6 7.0 %collective-permute-start.16 = (bf16[512,128]{1,0:T(8,128)(2,1)S(1)}, bf16[512,128]{1,0:T(8,128)(2,1)S(1)}, u32[]{:S(2)}, u32[]{:S(2)}) collective-permute-start(bf16[512,128]{1,0:T(8,128)(2,1)S(1)} %get-tuple-element.81), channel_id=1, source_target_pairs={{0,3},{1,0},{2,1},{3,2},{4,7},{5,4},{6,5},{7,6},{8,11},{9,8},{10,9... | collective-permute-start | bytes 393224 | tf_op jit(solution)/shard_map/ppermute | solution.py:392
  33.1 11.5 %copy-start.1 = (bf16[512,128]{1,0:T(8,128)(2,1)S(1)}, bf16[512,128]{1,0:T(8,128)(2,1)}, u32[]{:S(2)}) copy-start(bf16[512,128]{1,0:T(8,128)(2,1)} %grad_ref.1) | copy-start | bytes 393220
  33.1 11.5 %copy-start.2 = (bf16[128,128]{1,0:T(8,128)(2,1)S(1)}, bf16[128,128]{1,0:T(8,128)(2,1)}, u32[]{:S(2)}) copy-start(bf16[128,128]{1,0:T(8,128)(2,1)} %weight_ref.3) | copy-start | bytes 98308
  33.3 7.4 %collective-permute-start.9 = (bf16[512,128]{1,0:T(8,128)(2,1)S(1)}, bf16[512,128]{1,0:T(8,128)(2,1)S(1)}, u32[]{:S(2)}, u32[]{:S(2)}) collective-permute-start(bf16[512,128]{1,0:T(8,128)(2,1)S(1)} %get-tuple-element.73), channel_id=1, source_target_pairs={{0,1},{1,2},{2,3},{3,0},{4,5},{5,6},{6,7},{7,4},{8,9},{9,10},{10,1... | collective-permute-start | bytes 393224 | tf_op jit(solution)/shard_map/ppermute | solution.py:392
  34.8 6.2 %collective-permute-start.12 = (bf16[512,128]{1,0:T(8,128)(2,1)S(1)}, bf16[512,128]{1,0:T(8,128)(2,1)S(1)}, u32[]{:S(2)}, u32[]{:S(2)}) collective-permute-start(bf16[512,128]{1,0:T(8,128)(2,1)S(1)} %get-tuple-element.76), channel_id=1, source_target_pairs={{0,4},{1,5},{2,6},{3,7},{4,8},{5,9},{6,10},{7,11},{8,12},{9,13},{1... | collective-permute-start | bytes 393224 | tf_op jit(solution)/shard_map/ppermute | solution.py:388
  34.9 6.2 %collective-permute-start.13 = (bf16[512,128]{1,0:T(8,128)(2,1)S(1)}, bf16[512,128]{1,0:T(8,128)(2,1)S(1)}, u32[]{:S(2)}, u32[]{:S(2)}) collective-permute-start(bf16[512,128]{1,0:T(8,128)(2,1)S(1)} %get-tuple-element.77), channel_id=1, source_target_pairs={{0,12},{1,13},{2,14},{3,15},{4,0},{5,1},{6,2},{7,3},{8,4},{9,5},{1... | collective-permute-start | bytes 393224 | tf_op jit(solution)/shard_map/ppermute | solution.py:388
  37.6 5.9 %collective-permute-start.17 = (bf16[512,128]{1,0:T(8,128)(2,1)S(1)}, bf16[512,128]{1,0:T(8,128)(2,1)S(1)}, u32[]{:S(2)}, u32[]{:S(2)}) collective-permute-start(bf16[512,128]{1,0:T(8,128)(2,1)S(1)} %add_z.1), channel_id=1, source_target_pairs={{0,8},{1,9},{2,10},{3,11},{4,12},{5,13},{6,14},{7,15},{8,0},{9,1},... | collective-permute-start | bytes 393224 | tf_op jit(solution)/shard_map/ppermute | solution.py:388
  37.7 5.8 %collective-permute-start.10 = (bf16[512,128]{1,0:T(8,128)(2,1)S(1)}, bf16[512,128]{1,0:T(8,128)(2,1)S(1)}, u32[]{:S(2)}, u32[]{:S(2)}) collective-permute-start(bf16[512,128]{1,0:T(8,128)(2,1)S(1)} %get-tuple-element.74), channel_id=1, source_target_pairs={{0,2},{1,3},{2,0},{3,1},{4,6},{5,7},{6,4},{7,5},{8,10},{9,11},{10,... | collective-permute-start | bytes 393224 | tf_op jit(solution)/shard_map/ppermute | solution.py:392
  40.7 4.0 %collective-permute-start.11 = (bf16[512,128]{1,0:T(8,128)(2,1)S(1)}, bf16[512,128]{1,0:T(8,128)(2,1)S(1)}, u32[]{:S(2)}, u32[]{:S(2)}) collective-permute-start(bf16[512,128]{1,0:T(8,128)(2,1)S(1)} %get-tuple-element.75), channel_id=1, source_target_pairs={{0,3},{1,0},{2,1},{3,2},{4,7},{5,4},{6,5},{7,6},{8,11},{9,8},{10,9... | collective-permute-start | bytes 393224 | tf_op jit(solution)/shard_map/ppermute | solution.py:392
  45.7 6.7 %collective-permute-start.20 = (bf16[640,128]{1,0:T(8,128)(2,1)S(1)}, bf16[640,128]{1,0:T(8,128)(2,1)S(1)}, u32[]{:S(2)}, u32[]{:S(2)}) collective-permute-start(bf16[640,128]{1,0:T(8,128)(2,1)S(1)} %get-tuple-element.85.own.refs_0_), channel_id=1, source_target_pairs={{0,3},{1,0},{2,1},{3,2},{4,7},{5,4},{6,5},{7,6},{8,11},{9,8},{10,9... | collective-permute-start | bytes 491528 | tf_op jit(solution)/shard_map/ppermute | solution.py:392
  48.4 5.8 %collective-permute-start.19 = (bf16[640,128]{1,0:T(8,128)(2,1)S(1)}, bf16[640,128]{1,0:T(8,128)(2,1)S(1)}, u32[]{:S(2)}, u32[]{:S(2)}) collective-permute-start(bf16[640,128]{1,0:T(8,128)(2,1)S(1)} %get-tuple-element.85.own.refs_0_), channel_id=1, source_target_pairs={{0,2},{1,3},{2,0},{3,1},{4,6},{5,7},{6,4},{7,5},{8,10},{9,11},{10,... | collective-permute-start | bytes 491528 | tf_op jit(solution)/shard_map/ppermute | solution.py:392
  48.5 7.1 %collective-permute-start.18 = (bf16[640,128]{1,0:T(8,128)(2,1)S(1)}, bf16[640,128]{1,0:T(8,128)(2,1)S(1)}, u32[]{:S(2)}, u32[]{:S(2)}) collective-permute-start(bf16[640,128]{1,0:T(8,128)(2,1)S(1)} %get-tuple-element.85.own.refs_0_), channel_id=1, source_target_pairs={{0,1},{1,2},{2,3},{3,0},{4,5},{5,6},{6,7},{7,4},{8,9},{9,10},{10,1... | collective-permute-start | bytes 491528 | tf_op jit(solution)/shard_map/ppermute | solution.py:392
  48.9 8.3 %collective-permute-start.23 = (bf16[640,128]{1,0:T(8,128)(2,1)S(1)}, bf16[640,128]{1,0:T(8,128)(2,1)S(1)}, u32[]{:S(2)}, u32[]{:S(2)}) collective-permute-start(bf16[640,128]{1,0:T(8,128)(2,1)S(1)} %get-tuple-element.85.own.refs_0_), channel_id=1, source_target_pairs={{0,8},{1,9},{2,10},{3,11},{4,12},{5,13},{6,14},{7,15},{8,0},{9,1},... | collective-permute-start | bytes 491528 | tf_op jit(solution)/shard_map/ppermute | solution.py:388
  50.6 7.7 %collective-permute-start.22 = (bf16[640,128]{1,0:T(8,128)(2,1)S(1)}, bf16[640,128]{1,0:T(8,128)(2,1)S(1)}, u32[]{:S(2)}, u32[]{:S(2)}) collective-permute-start(bf16[640,128]{1,0:T(8,128)(2,1)S(1)} %get-tuple-element.85.own.refs_0_), channel_id=1, source_target_pairs={{0,12},{1,13},{2,14},{3,15},{4,0},{5,1},{6,2},{7,3},{8,4},{9,5},{1... | collective-permute-start | bytes 491528 | tf_op jit(solution)/shard_map/ppermute | solution.py:388
  52.4 7.4 %collective-permute-start.21 = (bf16[640,128]{1,0:T(8,128)(2,1)S(1)}, bf16[640,128]{1,0:T(8,128)(2,1)S(1)}, u32[]{:S(2)}, u32[]{:S(2)}) collective-permute-start(bf16[640,128]{1,0:T(8,128)(2,1)S(1)} %get-tuple-element.85.own.refs_0_), channel_id=1, source_target_pairs={{0,4},{1,5},{2,6},{3,7},{4,8},{5,9},{6,10},{7,11},{8,12},{9,13},{1... | collective-permute-start | bytes 491528 | tf_op jit(solution)/shard_map/ppermute | solution.py:388
  55.7 10.1 %collective-permute-start.28 = (bf16[1664,128]{1,0:T(8,128)(2,1)S(1)}, bf16[1664,128]{1,0:T(8,128)(2,1)S(1)}, u32[]{:S(2)}, u32[]{:S(2)}) collective-permute-start(bf16[1664,128]{1,0:T(8,128)(2,1)S(1)} %merge_z.1.refs_1_.rest), channel_id=1, source_target_pairs={{0,12},{1,13},{2,14},{3,15},{4,0},{5,1},{6,2},{7,3},{8,4},{9,5},{1... | collective-permute-start | bytes 1277960 | tf_op jit(solution)/shard_map/ppermute | solution.py:388
  56.9 11.0 %collective-permute-start.27 = (bf16[1664,128]{1,0:T(8,128)(2,1)S(1)}, bf16[1664,128]{1,0:T(8,128)(2,1)S(1)}, u32[]{:S(2)}, u32[]{:S(2)}) collective-permute-start(bf16[1664,128]{1,0:T(8,128)(2,1)S(1)} %merge_z.1.refs_1_.rest), channel_id=1, source_target_pairs={{0,4},{1,5},{2,6},{3,7},{4,8},{5,9},{6,10},{7,11},{8,12},{9,13},{1... | collective-permute-start | bytes 1277960 | tf_op jit(solution)/shard_map/ppermute | solution.py:388
  57.2 6.0 %collective-permute-start.26 = (bf16[640,128]{1,0:T(8,128)(2,1)S(1)}, bf16[640,128]{1,0:T(8,128)(2,1)S(1)}, u32[]{:S(2)}, u32[]{:S(2)}) collective-permute-start(bf16[640,128]{1,0:T(8,128)(2,1)S(1)} %collective-permute-done.23.refs_4_.level), channel_id=1, source_target_pairs={{0,3},{1,0},{2,1},{3,2},{4,7},{5,4},{6,5},{7,6},{8,11},{9,8},{10,9... | collective-permute-start | bytes 491528 | tf_op jit(solution)/shard_map/ppermute | solution.py:392
  58.3 5.7 %collective-permute-start.25 = (bf16[640,128]{1,0:T(8,128)(2,1)S(1)}, bf16[640,128]{1,0:T(8,128)(2,1)S(1)}, u32[]{:S(2)}, u32[]{:S(2)}) collective-permute-start(bf16[640,128]{1,0:T(8,128)(2,1)S(1)} %collective-permute-done.23.refs_4_.level), channel_id=1, source_target_pairs={{0,2},{1,3},{2,0},{3,1},{4,6},{5,7},{6,4},{7,5},{8,10},{9,11},{10,... | collective-permute-start | bytes 491528 | tf_op jit(solution)/shard_map/ppermute | solution.py:392
  59.8 5.9 %collective-permute-start.24 = (bf16[640,128]{1,0:T(8,128)(2,1)S(1)}, bf16[640,128]{1,0:T(8,128)(2,1)S(1)}, u32[]{:S(2)}, u32[]{:S(2)}) collective-permute-start(bf16[640,128]{1,0:T(8,128)(2,1)S(1)} %collective-permute-done.23.refs_4_.level), channel_id=1, source_target_pairs={{0,1},{1,2},{2,3},{3,0},{4,5},{5,6},{6,7},{7,4},{8,9},{9,10},{10,1... | collective-permute-start | bytes 491528 | tf_op jit(solution)/shard_map/ppermute | solution.py:392
  70.5 8.0 %collective-permute-start.29 = (f32[2176,128]{1,0:T(8,128)S(1)}, f32[2176,128]{1,0:T(8,128)S(1)}, u32[]{:S(2)}, u32[]{:S(2)}) collective-permute-start(f32[2176,128]{1,0:T(8,128)S(1)} %get-tuple-element.89), channel_id=1, source_target_pairs={{0,16},{16,0},{32,48},{48,32},{64,80},{80,64},{96,112},{112,96},{1... | collective-permute-start | bytes 3342344 | tf_op jit(solution)/shard_map/ppermute | solution.py:400
  78.6 10.6 %collective-permute-start.30 = (bf16[640,128]{1,0:T(8,128)(2,1)S(1)}, bf16[640,128]{1,0:T(8,128)(2,1)S(1)}, u32[]{:S(2)}, u32[]{:S(2)}) collective-permute-start(bf16[640,128]{1,0:T(8,128)(2,1)S(1)} %get-tuple-element.92), channel_id=1, source_target_pairs={{0,32},{16,48},{32,64},{48,80},{64,96},{80,112},{96,0},{112,16},{1... | collective-permute-start | bytes 491528 | tf_op jit(solution)/shard_map/ppermute | solution.py:396
  85.5 8.5 %collective-permute-start.31 = (bf16[640,128]{1,0:T(8,128)(2,1)S(1)}, bf16[640,128]{1,0:T(8,128)(2,1)S(1)}, u32[]{:S(2)}, u32[]{:S(2)}) collective-permute-start(bf16[640,128]{1,0:T(8,128)(2,1)S(1)} %get-tuple-element.93), channel_id=1, source_target_pairs={{0,64},{16,80},{32,96},{48,112},{64,0},{80,16},{96,32},{112,48},{1... | collective-permute-start | bytes 491528 | tf_op jit(solution)/shard_map/ppermute | solution.py:396
  86.0 8.1 %collective-permute-start.32 = (bf16[640,128]{1,0:T(8,128)(2,1)S(1)}, bf16[640,128]{1,0:T(8,128)(2,1)S(1)}, u32[]{:S(2)}, u32[]{:S(2)}) collective-permute-start(bf16[640,128]{1,0:T(8,128)(2,1)S(1)} %get-tuple-element.94), channel_id=1, source_target_pairs={{0,96},{16,112},{32,0},{48,16},{64,32},{80,48},{96,64},{112,80},{1... | collective-permute-start | bytes 491528 | tf_op jit(solution)/shard_map/ppermute | solution.py:396
